TPU v7x, 128 devices: a whole 4x4x4 slice. The times are simulated.
128 devices in a mesh: section: 2 (over x_lo), replica: 4 (over x_hi, core), shard: 16 (over z, y).
Axes of the slice: x: 4 (x_hi: 2, x_lo: 2; x = x_hi * 2 + x_lo), y: 4, z: 4, core: 2. Of those that a mesh axis runs over, the one named last changes fastest.
Arguments:
- layer_input: bfloat16 [2, 64, 128, 1024], P(None, ('replica', 'shard')), may hold values from -6 to 6
- cotangent: bfloat16 [2, 64, 128, 1024], P(None, ('replica', 'shard')), may hold values from -6 to 6
- project_weight: bfloat16 [2, 1024, 3072], P('section', 'shard'), may hold values from -0.1875 to 0.1875
- output_weight: bfloat16 [2, 1024, 1024], P('section', 'shard'), may hold values from -0.5 to 0.5
- up_weight: bfloat16 [2, 1024, 4096], P('section', 'shard'), may hold values from -0.1875 to 0.1875
- down_weight: bfloat16 [2, 4096, 1024], P('section', 'shard'), may hold values from -0.09375 to 0.09375
- query_bias: bfloat16 [2, 1024], P('section', 'shard'), may hold values from -3 to 3
- value_bias: bfloat16 [2, 1024], P('section', 'shard'), may hold values from -3 to 3
- output_bias: bfloat16 [2, 1024], P('section', 'shard'), may hold values from -3 to 3
- up_bias: bfloat16 [2, 4096], P('section', 'shard'), may hold values from -3 to 3
- down_bias: bfloat16 [2, 1024], P('section', 'shard'), may hold values from -3 to 3
- first_gain: bfloat16 [2, 1024], P('section', 'shard'), may hold values from 0.5 to 1.5
- first_shift: bfloat16 [2, 1024], P('section', 'shard'), may hold values from -2 to 2
- second_gain: bfloat16 [2, 1024], P('section', 'shard'), may hold values from 0.5 to 1.5
- second_shift: bfloat16 [2, 1024], P('section', 'shard'), may hold values from -2 to 2
Outputs:
- layer_output: bfloat16 [2, 2, 64, 128, 1024], P('section', None, ('replica', 'shard'))
- input_grad: bfloat16 [2, 2, 64, 128, 1024], P('section', None, ('replica', 'shard'))
- project_grad: float32 [2, 1024, 3072], P('section', 'shard')
- output_grad: float32 [2, 1024, 1024], P('section', 'shard')
- up_grad: float32 [2, 1024, 4096], P('section', 'shard')
- down_grad: float32 [2, 4096, 1024], P('section', 'shard')
- query_bias_grad: float32 [2, 1024], P('section', 'shard')
- value_bias_grad: float32 [2, 1024], P('section', 'shard')
- output_bias_grad: float32 [2, 1024], P('section', 'shard')
- up_bias_grad: float32 [2, 4096], P('section', 'shard')
- down_bias_grad: float32 [2, 1024], P('section', 'shard')
- first_gain_grad: float32 [2, 1024], P('section', 'shard')
- first_shift_grad: float32 [2, 1024], P('section', 'shard')
- second_gain_grad: float32 [2, 1024], P('section', 'shard')
- second_shift_grad: float32 [2, 1024], P('section', 'shard')
All inputs are finite; a program needn't handle non-finite values.
Results may differ from a plain program's by a relative error of at most 0.02.
Values may be sent and summed in bfloat16 or wider, within the bound.
No kernel may reach another device: no remote copies, remote signals or barrier semaphores. Data moves between devices by JAX's collectives and lax.ppermute only.
A program may use at most 192 MiB of HBM per device.

v0:
```python
import jax
import jax.numpy as jnp
from jax import lax
from jax.sharding import PartitionSpec as P

HEADS = 16
HEAD_DIM = 64
LEN = 128


EPSILON = 1e-06


def side_by_side(arrays, axis, dim, along):
    widths = [a.shape[along] for a in arrays]
    both = jnp.concatenate(arrays, axis=along)
    whole = lax.all_gather(both, axis, axis=dim, tiled=True)
    return tuple(jnp.split(whole, [sum(widths[:k]) for k in range(1, len(widths))], axis=along))


def from_behind(value, axis, steps):
    count = lax.axis_size(axis)
    leading, last = (max(0, -steps), min(count, count - steps))
    return lax.ppermute(value, axis, [(source, source + steps) for source in range(leading, last)])


def in_one_piece(arrays, axis, dim, along):
    ends, at = ([], 0)
    for a in arrays[:-1]:
        at += a.shape[along]
        ends.append(at)
    both = jnp.concatenate(arrays, axis=along)
    return tuple(
        jnp.split(lax.psum_scatter(both, axis, scatter_dimension=dim, tiled=True), ends, axis=along)
    )


def total_of_pieces(shard, axis):
    return lax.all_gather(shard, axis).astype(jnp.float32).sum(0)


def matmul(left, right):
    return jnp.dot(left, right, preferred_element_type=jnp.float32)


def matmul_back(left, right):
    return lax.dot_general(
        left, right, (((1,), (1,)), ((), ())), preferred_element_type=jnp.float32
    )


def matmul_rows(left, right):
    return lax.dot_general(
        left, right, (((0,), (0,)), ((), ())), preferred_element_type=jnp.float32
    )


def gelu_exact(values):
    return jax.nn.gelu(values, approximate=False)


def unpack(gathered):
    return tuple((piece[0] for piece in gathered))


def norm_forward(totals, gain_row, shift_row):
    average = jnp.mean(totals, -1, keepdims=True)
    centred = totals - average
    inverse = lax.rsqrt(jnp.mean(centred * centred, -1, keepdims=True) + EPSILON)
    normed = centred * inverse
    return (normed * gain_row.astype(jnp.float32) + shift_row.astype(jnp.float32), normed, inverse)


def norm_backward(upstream, normed, inverse, gain_row):
    scaled = upstream * gain_row.astype(jnp.float32)
    return inverse * (
        scaled
        - jnp.mean(scaled, -1, keepdims=True)
        - normed * jnp.mean(scaled * normed, -1, keepdims=True)
    )


def split_heads(packed):
    return packed.reshape(-1, LEN, 3, HEADS, HEAD_DIM)


def layer_forward(rows16, weights):
    (
        project,
        output,
        upward,
        downward,
        query_row,
        value_row,
        output_row,
        up_row,
        down_row,
        gain_one,
        shift_one,
        gain_two,
        shift_two,
    ) = unpack(weights)
    width = output.shape[0]
    biases = jnp.concatenate(
        [
            query_row.astype(jnp.float32),
            jnp.zeros((width,), jnp.float32),
            value_row.astype(jnp.float32),
        ]
    )
    packed = (matmul(rows16, project) + biases).astype(jnp.bfloat16)
    heads_view = split_heads(packed)
    scores = jnp.einsum(
        "sqhe,skhe->shqk",
        heads_view[:, :, 0],
        heads_view[:, :, 1],
        preferred_element_type=jnp.float32,
    ) * HEAD_DIM ** (-0.5)
    log_totals = jax.nn.logsumexp(scores, axis=-1, keepdims=True)
    soft16 = jnp.exp(scores - log_totals).astype(jnp.bfloat16)
    attended = (
        jnp.einsum(
            "shqk,skhe->sqhe", soft16, heads_view[:, :, 2], preferred_element_type=jnp.float32
        )
        .reshape(-1, width)
        .astype(jnp.bfloat16)
    )
    residual_one = rows16.astype(jnp.float32) + (
        matmul(attended, output) + output_row.astype(jnp.float32)
    )
    hidden, normed_one, inverse_one = norm_forward(residual_one, gain_one, shift_one)
    hidden16 = hidden.astype(jnp.bfloat16)
    upper = matmul(hidden16, upward) + up_row.astype(jnp.float32)
    active16 = gelu_exact(upper).astype(jnp.bfloat16)
    residual_two = hidden + (matmul(active16, downward) + down_row.astype(jnp.float32))
    result, normed_two, inverse_two = norm_forward(residual_two, gain_two, shift_two)
    kept = (
        rows16,
        packed,
        log_totals,
        attended,
        normed_one,
        inverse_one,
        hidden16,
        upper,
        active16,
        normed_two,
        inverse_two,
    )
    return (result, kept)


def layer_backward(upstream, kept, weights, valid):
    (
        project,
        output,
        upward,
        downward,
        query_row,
        value_row,
        output_row,
        up_row,
        down_row,
        gain_one,
        shift_one,
        gain_two,
        shift_two,
    ) = unpack(weights)
    (
        rows16,
        packed,
        log_totals,
        attended,
        normed_one,
        inverse_one,
        hidden16,
        upper,
        active16,
        normed_two,
        inverse_two,
    ) = kept
    width = output.shape[0]
    scale = HEAD_DIM ** (-0.5)
    gain_two_grad = jnp.sum(upstream * normed_two, 0)
    shift_two_grad = jnp.sum(upstream, 0)
    total_two_grad = norm_backward(upstream, normed_two, inverse_two, gain_two)
    down_grad16 = total_two_grad.astype(jnp.bfloat16)
    active_grad = matmul_back(down_grad16, downward)
    upper_grad16 = jax.vjp(gelu_exact, upper)[1](active_grad)[0].astype(jnp.bfloat16)
    hidden_grad = matmul_back(upper_grad16, upward) + total_two_grad
    gain_one_grad = jnp.sum(hidden_grad * normed_one, 0)
    shift_one_grad = jnp.sum(hidden_grad, 0)
    total_grad = norm_backward(hidden_grad, normed_one, inverse_one, gain_one)
    branch_grad16 = total_grad.astype(jnp.bfloat16)
    attended_grad16 = (
        matmul_back(branch_grad16, output).astype(jnp.bfloat16).reshape(-1, LEN, HEADS, HEAD_DIM)
    )
    heads_view = split_heads(packed)
    queries = heads_view[:, :, 0]
    keys_all = heads_view[:, :, 1]
    values_all = heads_view[:, :, 2]
    scores = (
        jnp.einsum("sqhe,skhe->shqk", queries, keys_all, preferred_element_type=jnp.float32) * scale
    )
    soft = jnp.exp(scores - log_totals)
    soft16 = soft.astype(jnp.bfloat16)
    values_grad = jnp.einsum(
        "shqk,sqhe->skhe", soft16, attended_grad16, preferred_element_type=jnp.float32
    )
    soft_grad = jnp.einsum(
        "sqhe,skhe->shqk", attended_grad16, values_all, preferred_element_type=jnp.float32
    )
    scores_grad16 = (soft * (soft_grad - jnp.sum(soft_grad * soft, -1, keepdims=True))).astype(
        jnp.bfloat16
    )
    queries_grad = (
        jnp.einsum("shqk,skhe->sqhe", scores_grad16, keys_all, preferred_element_type=jnp.float32)
        * scale
    )
    keys_grad = (
        jnp.einsum("shqk,sqhe->skhe", scores_grad16, queries, preferred_element_type=jnp.float32)
        * scale
    )
    packed_grad16 = (
        jnp.stack([queries_grad, keys_grad, values_grad], 2)
        .reshape(-1, 3 * width)
        .astype(jnp.bfloat16)
    )
    rows_grad = matmul_back(packed_grad16, project) + total_grad
    packed_grad16 = jnp.where(valid, packed_grad16, jnp.zeros_like(packed_grad16))
    branch_grad16 = jnp.where(valid, branch_grad16, jnp.zeros_like(branch_grad16))
    upper_grad16 = jnp.where(valid, upper_grad16, jnp.zeros_like(upper_grad16))
    down_grad16 = jnp.where(valid, down_grad16, jnp.zeros_like(down_grad16))
    packed_sums = jnp.sum(packed_grad16.astype(jnp.float32), 0)
    vector_grads = (
        packed_sums[:width],
        packed_sums[2 * width :],
        jnp.sum(branch_grad16.astype(jnp.float32), 0),
        jnp.sum(upper_grad16.astype(jnp.float32), 0),
        jnp.sum(down_grad16.astype(jnp.float32), 0),
        jnp.where(valid, gain_one_grad, 0.0),
        jnp.where(valid, shift_one_grad, 0.0),
        jnp.where(valid, gain_two_grad, 0.0),
        jnp.where(valid, shift_two_grad, 0.0),
    )
    pieces = (
        rows16,
        packed_grad16,
        attended,
        branch_grad16,
        hidden16,
        upper_grad16,
        active16,
        down_grad16,
    )
    return (rows_grad, pieces, vector_grads)


def on_device(
    layer_input,
    cotangent,
    project_weight,
    output_weight,
    up_weight,
    down_weight,
    query_bias,
    value_bias,
    output_bias,
    up_bias,
    down_bias,
    first_gain,
    first_shift,
    second_gain,
    second_shift,
):
    micro = layer_input.shape[0]
    local_seqs = layer_input.shape[1]
    width = layer_input.shape[3]
    first_section = lax.axis_index("section") == 0
    received = jnp.zeros((local_seqs * LEN, width), jnp.bfloat16)
    results = []
    kept_ticks = []
    for step_index in range(micro + 1):
        gathered = (
            *side_by_side((project_weight, output_weight, up_weight), "shard", 1, 2),
            lax.all_gather(down_weight, "shard", axis=1, tiled=True),
            *side_by_side((query_bias, value_bias, output_bias), "shard", 1, 0),
            lax.all_gather(up_bias, "shard", axis=1, tiled=True),
            *side_by_side(
                (down_bias, first_gain, first_shift, second_gain, second_shift), "shard", 1, 0
            ),
        )
        own_rows = layer_input[min(step_index, micro - 1)].reshape(-1, width)
        layer_rows = jnp.where(first_section, own_rows, received)
        result, kept = layer_forward(layer_rows, gathered)
        result16 = result.astype(jnp.bfloat16)
        results.append(result16)
        kept_ticks.append(kept)
        if step_index < micro:
            received = from_behind(result16, "section", 1)
    layer_output = jnp.stack(
        [jnp.where(first_section, results[index], results[index + 1]) for index in range(micro)]
    ).reshape(1, micro, local_seqs, LEN, width)
    back_received = jnp.zeros((local_seqs * LEN, width), jnp.bfloat16)
    rows_grads = []
    piece_ticks = []
    vector_total = None
    for step_index in range(micro + 1):
        gathered = (
            *side_by_side((project_weight, output_weight, up_weight), "shard", 1, 2),
            lax.all_gather(down_weight, "shard", axis=1, tiled=True),
            *side_by_side((query_bias, value_bias, output_bias), "shard", 1, 0),
            lax.all_gather(up_bias, "shard", axis=1, tiled=True),
            *side_by_side(
                (down_bias, first_gain, first_shift, second_gain, second_shift), "shard", 1, 0
            ),
        )
        own_grad = cotangent[min(step_index, micro - 1)].reshape(-1, width)
        upstream = jnp.where(first_section, back_received, own_grad).astype(jnp.float32)
        kept = jax.tree.map(
            lambda early, later: jnp.where(first_section, early, later),
            kept_ticks[max(step_index - 1, 0)],
            kept_ticks[min(step_index + 1, micro)],
        )
        valid = jnp.where(first_section, step_index >= 1, step_index < micro)
        rows_grad, pieces, vector_grads = layer_backward(upstream, kept, gathered, valid)
        rows_grad16 = rows_grad.astype(jnp.bfloat16)
        rows_grads.append(rows_grad16)
        piece_ticks.append(pieces)
        if vector_total is None:
            vector_total = vector_grads
        else:
            vector_total = tuple(
                (total + extra for total, extra in zip(vector_total, vector_grads))
            )
        if step_index < micro:
            back_received = from_behind(rows_grad16, "section", -1)
    input_grad = jnp.stack(
        [
            jnp.where(first_section, rows_grads[index + 1], rows_grads[index])
            for index in range(micro)
        ]
    ).reshape(1, micro, local_seqs, LEN, width)
    joined = [jnp.concatenate([pieces[column] for pieces in piece_ticks]) for column in range(8)]
    gradients = [
        matmul_rows(joined[0], joined[1]),
        matmul_rows(joined[2], joined[3]),
        matmul_rows(joined[4], joined[5]),
        matmul_rows(joined[6], joined[7]),
    ]
    gradients = [matrix[None] for matrix in gradients] + [vector[None] for vector in vector_total]
    owned = (
        *tuple(
            (
                part.astype(jnp.float32)
                for part in in_one_piece(
                    (
                        gradients[0].astype(jnp.bfloat16),
                        gradients[1].astype(jnp.bfloat16),
                        gradients[2].astype(jnp.bfloat16),
                    ),
                    "shard",
                    1,
                    2,
                )
            )
        ),
        lax.psum_scatter(
            gradients[3].astype(jnp.bfloat16), "shard", scatter_dimension=1, tiled=True
        ).astype(jnp.float32),
        *tuple(
            (
                part.astype(jnp.float32)
                for part in in_one_piece(
                    (
                        gradients[4].astype(jnp.bfloat16),
                        gradients[5].astype(jnp.bfloat16),
                        gradients[6].astype(jnp.bfloat16),
                    ),
                    "shard",
                    1,
                    0,
                )
            )
        ),
        lax.psum_scatter(
            gradients[7].astype(jnp.bfloat16), "shard", scatter_dimension=1, tiled=True
        ).astype(jnp.float32),
        *tuple(
            (
                part.astype(jnp.float32)
                for part in in_one_piece(
                    (
                        gradients[8].astype(jnp.bfloat16),
                        gradients[9].astype(jnp.bfloat16),
                        gradients[10].astype(jnp.bfloat16),
                        gradients[11].astype(jnp.bfloat16),
                        gradients[12].astype(jnp.bfloat16),
                    ),
                    "shard",
                    1,
                    0,
                )
            )
        ),
    )
    finals = (
        total_of_pieces(owned[0].astype(jnp.bfloat16), "replica").astype(jnp.float32),
        total_of_pieces(owned[1].astype(jnp.bfloat16), "replica").astype(jnp.float32),
        total_of_pieces(owned[2].astype(jnp.bfloat16), "replica").astype(jnp.float32),
        total_of_pieces(owned[3].astype(jnp.bfloat16), "replica").astype(jnp.float32),
        total_of_pieces(owned[4].astype(jnp.bfloat16), "replica").astype(jnp.float32),
        total_of_pieces(owned[5].astype(jnp.bfloat16), "replica").astype(jnp.float32),
        total_of_pieces(owned[6].astype(jnp.bfloat16), "replica").astype(jnp.float32),
        total_of_pieces(owned[7].astype(jnp.bfloat16), "replica").astype(jnp.float32),
        total_of_pieces(owned[8].astype(jnp.bfloat16), "replica").astype(jnp.float32),
        total_of_pieces(owned[9].astype(jnp.bfloat16), "replica").astype(jnp.float32),
        total_of_pieces(owned[10].astype(jnp.bfloat16), "replica").astype(jnp.float32),
        total_of_pieces(owned[11].astype(jnp.bfloat16), "replica").astype(jnp.float32),
        total_of_pieces(owned[12].astype(jnp.bfloat16), "replica").astype(jnp.float32),
    )
    return (
        layer_output,
        input_grad,
        finals[0],
        finals[1],
        finals[2],
        finals[3],
        finals[4],
        finals[5],
        finals[6],
        finals[7],
        finals[8],
        finals[9],
        finals[10],
        finals[11],
        finals[12],
    )


def solution(mesh):
    placed = (
        P(None, ("replica", "shard"), None, None),
        P(None, ("replica", "shard"), None, None),
        P("section", "shard", None),
        P("section", "shard", None),
        P("section", "shard", None),
        P("section", "shard", None),
        P("section", "shard"),
        P("section", "shard"),
        P("section", "shard"),
        P("section", "shard"),
        P("section", "shard"),
        P("section", "shard"),
        P("section", "shard"),
        P("section", "shard"),
        P("section", "shard"),
    )
    return jax.shard_map(
        on_device,
        mesh=mesh,
        in_specs=placed,
        out_specs=(
            P("section", None, ("replica", "shard"), None, None),
            P("section", None, ("replica", "shard"), None, None),
            P("section", "shard", None),
            P("section", "shard", None),
            P("section", "shard", None),
            P("section", "shard", None),
            P("section", "shard"),
            P("section", "shard"),
            P("section", "shard"),
            P("section", "shard"),
            P("section", "shard"),
            P("section", "shard"),
            P("section", "shard"),
            P("section", "shard"),
            P("section", "shard"),
        ),
        check_vma=False,
    )
```

profile of v0, /device:TPU:1, one launch (start us, length us, event | category | flops | bytes accessed | tf_op | source)
XLA Modules:
  0.0 878.2 jit_solution(15639767721339765553)
XLA Ops:
  7.3 2.3 pad_maximum_fusion.1
  10.6 20.9 %all-gather.14 = bf16[16,64,5]{1,2,0:T(8,128)(2,1)S(1)} all-gather(bf16[1,64,5]{1,2,0:T(8,128)(2,1)S(1)} %bitcast.541), channel_id=1, replica_groups=mesh['section'=2,'replica'=4,'shard'=16] {'shard'}, dimensions={0}, use_global_device_ids=true | all-gather | bytes 10880 | tf_op jit(solution)/shard_map/all_gather | solution.py:17
  31.6 18.8 %all_gather.115 = bf16[1,4096]{1,0:T(2,128)(2,1)S(1)} all-gather(bf16[1,256]{1,0:T(2,128)(2,1)S(1)} %copy-done.85), channel_id=1, replica_groups=mesh['section'=2,'replica'=4,'shard'=16] {'shard'}, dimensions={1}, use_global_device_ids=true | all-gather | bytes 8704 | tf_op jit(solution)/shard_map/all_gather | solution.py:288
  50.5 17.3 %all-gather.13 = bf16[16,64,3]{1,2,0:T(4,128)(2,1)S(1)} all-gather(bf16[1,64,3]{1,2,0:T(4,128)(2,1)S(1)} %maximum_bitcast_fusion.2), channel_id=1, replica_groups=mesh['section'=2,'replica'=4,'shard'=16] {'shard'}, dimensions={0}, use_global_device_ids=true | all-gather | bytes 6528 | tf_op jit(solution)/shard_map/all_gather | solution.py:17
  68.0 57.8 %all-gather.30.cloned.1.call-done = bf16[1,1024,8192]{2,1,0:T(8,128)(2,1)} async-done(((bf16[1,64,8192]{2,1,0:T(8,128)(2,1)}), bf16[1,1024,8192]{2,1,0:T(8,128)(2,1)}) %all-gather.30.cloned.1.call-update) | async-done | bytes 16777232 | tf_op jit(solution)/shard_map/all_gather | solution.py:17
  125.8 3.8 fusion.12
  130.9 2.2 fusion.252
  133.3 9.1 %fusion.38 = (bf16[128,4096]{1,0:T(8,128)(2,1)S(1)}, f32[128,4096]{1,0:T(8,128)}) fusion(f32[4096]{0:T(1024)S(1)} %bitcast.536, bf16[1,1024,8192]{2,1,0:T(8,128)(2,1)} %all-gather.30.cloned.1.call-done, f32[128,1024]{1,0:T(8,128)S(1)} %get-tuple-element.178, f32[1024]{0:T(1024)S(1)} %bitcast.518, f32[1024]{0:T(1024)S(1)} %bitcast.500, ...), kind=kOutput, calls=%fused_computation.59 | convolution fusion | flops 1109000192 | bytes 12084224 | tf_op jit(solution)/shard_map/dot_general | solution.py:43
  142.4 56.0 %all-gather.32.cloned.1.call-done = bf16[1,4096,1024]{2,1,0:T(8,128)(2,1)} async-done(((bf16[1,256,1024]{2,1,0:T(8,128)(2,1)}), bf16[1,4096,1024]{2,1,0:T(8,128)(2,1)}) %all-gather.32.cloned.1.call-update) | async-done | bytes 8388624 | tf_op jit(solution)/shard_map/all_gather | solution.py:286
  198.4 4.8 fusion.253
  203.6 3.3 collective-permute-start
  207.0 4.7 collective-permute-done
  212.4 4.7 fusion.13
  217.1 2.3 copy.99
  222.2 2.1 fusion.255
  225.6 9.7 %broadcast_select_fusion.3 = (bf16[128,4096]{1,0:T(8,128)(2,1)}, bf16[128,4096]{1,0:T(8,128)(2,1)S(1)}, f32[128,4096]{1,0:T(8,128)}) fusion(bf16[128,4096]{1,0:T(8,128)(2,1)S(1)} %get-tuple-element.179, pred[]{:T(512)S(6)} %eq.3, f32[4096]{0:T(1024)S(1)} %bitcast.537, bf16[128,1024]{1,0:T(8,128)(2,1)S(1)} %get-tuple-element.120, ...), kind=kOutput, calls=%fused_computation.254 | convolution fusion | flops 1108869120 | bytes 13910017 | tf_op jit(solution)/shard_map/dot_general | solution.py:43
  238.1 4.4 collective-permute-start.1
  242.5 1.6 fusion.183
  247.0 5.6 broadcast_select_fusion.7
  252.6 2.3 copy.101
  256.5 2.0 broadcast_select_fusion.14
  258.6 2.3 fusion.258
  262.6 9.4 %broadcast_select_fusion.2 = (bf16[128,4096]{1,0:T(8,128)(2,1)}, bf16[128,4096]{1,0:T(8,128)(2,1)S(1)}, f32[128,4096]{1,0:T(8,128)}) fusion(bf16[128,4096]{1,0:T(8,128)(2,1)S(1)} %get-tuple-element.179, pred[]{:T(512)S(6)} %eq.3, f32[4096]{0:T(1024)S(1)} %bitcast.538, bf16[128,1024]{1,0:T(8,128)(2,1)S(1)} %get-tuple-element.122, ...), kind=kOutput, calls=%fused_computation.253 | convolution fusion | flops 1108869120 | bytes 13910017 | tf_op jit(solution)/shard_map/dot_general | solution.py:43
  274.0 12.1 %convert_reduce_fusion.5 = (f32[4096]{0:T(1024)S(1)}, bf16[128,4096]{1,0:T(8,128)(2,1)}, bf16[128,4096]{1,0:T(8,128)(2,1)}) fusion(pred[]{:T(512)S(6)} %select_n.556, bf16[1,4096,1024]{2,1,0:T(8,128)(2,1)S(1)} %bitcast.443, f32[128,1024]{1,0:T(8,128)S(1)} %copy-done.19, f32[128]{0:T(128)S(1)} %copy-done.86, f32[128]{0:T(128)S(1)} %copy-done.88, ...), kind=kOutput, calls=%fused_computation.84 | convolution fusion | flops 1114632192 | bytes 15490048 | tf_op jit(solution)/shard_map/dot_general | solution.py:47
  286.2 5.0 multiply_reduce_fusion.5
  298.9 5.8 fusion.141
  308.8 3.5 collective-permute-done.2
  312.4 2.5 convert_reduce_fusion.15
  315.1 10.8 %convert_reduce_fusion.4 = (f32[4096]{0:T(1024)}, bf16[128,4096]{1,0:T(8,128)(2,1)S(1)}) fusion(f32[128,4096]{1,0:T(8,128)} %get-tuple-element.180, f32[128,4096]{1,0:T(8,128)} %get-tuple-element.194, pred[]{:T(512)S(6)} %eq.3, bf16[128,1024]{1,0:T(8,128)(2,1)S(1)} %get-tuple-element.84, bf16[1,4096,1024]{2,1,0:T(8,128)(2,1)} %all-gather.32.cloned.1.call-done), kind=kOutput, calls=%fused_computation.83 | convolution fusion | flops 1113059328 | bytes 13910017 | tf_op jit(solution)/shard_map/dot_general | solution.py:47
  326.0 3.6 multiply_reduce_fusion.4
  335.1 5.3 fusion.140
  342.1 5.6 collective-permute-done.3
  349.1 7.0 convert_bitcast_fusion
  359.7 11.5 %convert_reduce_fusion.3 = (f32[4096]{0:T(1024)}, bf16[128,4096]{1,0:T(8,128)(2,1)}, bf16[128,4096]{1,0:T(8,128)(2,1)S(1)}) fusion(pred[]{:T(512)S(6)} %eq.3, bf16[1,4096,1024]{2,1,0:T(8,128)(2,1)} %all-gather.32.cloned.1.call-done, f32[128,1024]{1,0:T(8,128)S(1)} %copy-done.21, f32[128]{0:T(128)S(1)} %broadcast_multiply_fusion.2, f32[128]{0:T(128)S(1)} %copy-done.91, ...), kind=kOutput, calls=%fused_computation.82 | convolution fusion | flops 1114501120 | bytes 15488513 | tf_op jit(solution)/shard_map/dot_general | solution.py:47
  371.3 6.2 multiply_reduce_fusion.3
  379.1 3.2 convolution_convert_fusion
  383.5 3.9 convert_bitcast_fusion.3
  387.3 4.0 copy.118
  394.5 3.7 convert_bitcast_fusion.2
  398.3 7.2 convert_bitcast_fusion.1
  405.5 6.6 pad_maximum_fusion
  413.5 1.6 reshape_bitcast_fusion
  416.4 27.0 %reduce-scatter.14.cloned.1.call-done = bf16[1,256,1024]{2,1,0:T(8,128)(2,1)} async-done(((bf16[1,4096,1024]{2,1,0:T(8,128)(2,1)}), bf16[1,256,1024]{2,1,0:T(8,128)(2,1)}) %reduce-scatter.14.cloned.1.call-update) | async-done | bytes 524304 | tf_op jit(solution)/shard_map/reduce_scatter | solution.py:368
  443.5 114.1 %reduce-scatter.12.cloned.1.call-done = bf16[1,64,8192]{2,1,0:T(8,128)(2,1)} async-done(((bf16[1,1024,8192]{2,1,0:T(8,128)(2,1)}), bf16[1,64,8192]{2,1,0:T(8,128)(2,1)}) %reduce-scatter.12.cloned.1.call-update) | async-done | bytes 1048592 | tf_op jit(solution)/shard_map/reduce_scatter | solution.py:34
  557.6 1.9 split.136
  561.5 5.1 fusion.143
  567.4 64.1 %reduce-scatter.16.cloned.1.call-done = bf16[64,3]{1,0:T(8,128)(2,1)} async-done(((bf16[1024,3]{1,0:T(8,128)(2,1)}), bf16[64,3]{1,0:T(8,128)(2,1)}) %reduce-scatter.16.cloned.1.call-update) | async-done | bytes 400
  632.7 8.7 all-gather.15
  641.3 6.5 all-gather.16
  647.9 6.5 all-gather.17
  656.0 51.9 %reduce-scatter.18.cloned.1.call-done = bf16[256,1]{1,0:T(8,128)(2,1)} async-done(((bf16[4096,1]{1,0:T(8,128)(2,1)}), bf16[256,1]{1,0:T(8,128)(2,1)}) %reduce-scatter.18.cloned.1.call-update) | async-done | bytes 528
  708.8 8.7 all-gather.18
  718.0 64.3 %reduce-scatter.20.cloned.1.call-done = bf16[64,5]{1,0:T(8,128)(2,1)} async-done(((bf16[1024,5]{1,0:T(8,128)(2,1)}), bf16[64,5]{1,0:T(8,128)(2,1)}) %reduce-scatter.20.cloned.1.call-update) | async-done | bytes 656
  783.7 8.7 all-gather.19
  792.4 6.5 all-gather.20
  798.9 6.5 all-gather.21
  805.4 6.5 all-gather.22
  812.0 6.5 all-gather.23
  821.2 3.2 convert_reduce_fusion
  824.3 12.0 %all-gather.1 = bf16[4,64,1024]{2,1,0:T(8,128)(2,1)S(1)} all-gather(bf16[1,64,1024]{2,1,0:T(8,128)(2,1)S(1)} %slice-done.12), channel_id=3, replica_groups=mesh['section'=2,'replica'=4,'shard'=16] {'replica'}, dimensions={0}, use_global_device_ids=true | all-gather | bytes 655360 | tf_op jit(solution)/shard_map/all_gather | solution.py:39
  837.1 2.6 all-gather.34.cloned.1.call-done
  839.7 2.6 convert_reduce_fusion.2
  842.3 25.7 %all-gather.36.cloned.1.call-done = bf16[4,64,4096]{2,1,0:T(8,128)(2,1)} async-done(((bf16[1,64,4096]{2,1,0:T(8,128)(2,1)}), bf16[4,64,4096]{2,1,0:T(8,128)(2,1)}) %all-gather.36.cloned.1.call-update) | async-done | bytes 2097168 | tf_op jit(solution)/shard_map/all_gather | solution.py:39
  868.0 3.0 convert_reduce_fusion.1
  (410 shorter events, 62.6 us)
Async XLA Ops:
  7.2 24.4 %copy-start.85 = (bf16[1,256]{1,0:T(2,128)(2,1)S(1)}, bf16[1,256]{1,0:T(2,128)(2,1)}, u32[]{:S(2)}) copy-start(bf16[1,256]{1,0:T(2,128)(2,1)} %param.24) | copy-start | bytes 1540
  7.2 43.2 %copy-start.97 = (bf16[1,64]{1,0:T(2,128)(2,1)S(1)}, bf16[1,64]{1,0:T(2,128)(2,1)}, u32[]{:S(2)}) copy-start(bf16[1,64]{1,0:T(2,128)(2,1)} %param.23) | copy-start | bytes 388
  7.3 43.2 %copy-start.98 = (bf16[1,64]{1,0:T(2,128)(2,1)S(1)}, bf16[1,64]{1,0:T(2,128)(2,1)}, u32[]{:S(2)}) copy-start(bf16[1,64]{1,0:T(2,128)(2,1)} %param.22) | copy-start | bytes 388
  7.3 43.2 %copy-start.99 = (bf16[1,64]{1,0:T(2,128)(2,1)S(1)}, bf16[1,64]{1,0:T(2,128)(2,1)}, u32[]{:S(2)}) copy-start(bf16[1,64]{1,0:T(2,128)(2,1)} %param.21) | copy-start | bytes 388
  7.3 118.5 %copy-start.17 = (bf16[2,1,128,1024]{3,2,1,0:T(8,128)(2,1)S(1)}, bf16[2,1,128,1024]{3,2,1,0:T(8,128)(2,1)}, u32[]{:S(2)}) copy-start(bf16[2,1,128,1024]{3,2,1,0:T(8,128)(2,1)} %param.15) | copy-start | bytes 1572868
  7.3 118.5 %all-gather.30.cloned.1.call-start = ((), (), s32[]{:S(2)}) async-start(), calls=%async_computation.5 | async-start | bytes 17825792 | tf_op jit(solution)/shard_map/all_gather | solution.py:17
  9.7 188.8 %all-gather.32.cloned.1.call-start = ((), (), s32[]{:S(2)}) async-start(), calls=%async_computation.6 | async-start | bytes 8912896 | tf_op jit(solution)/shard_map/all_gather | solution.py:286
  10.4 433.0 %reduce-scatter.14.cloned.1.call-start = ((), (), s32[]{:S(2)}) async-start(), calls=%async_computation.8 | async-start | bytes 8912896 | tf_op jit(solution)/shard_map/reduce_scatter | solution.py:368
  68.0 169.0 %copy-start.62 = (f32[1,1024]{1,0:T(1,128)}, f32[1,1024]{1,0:T(1,128)S(1)}, u32[]{:S(2)}) copy-start(f32[1,1024]{1,0:T(1,128)S(1)} %get-tuple-element.160) | copy-start | bytes 12292
  203.6 8.1 collective-permute-start
  224.4 11.0 %copy-start.1 = (f32[128,1024]{1,0:T(8,128)}, f32[128,1024]{1,0:T(8,128)S(1)}, u32[]{:S(2)}) copy-start(f32[128,1024]{1,0:T(8,128)S(1)} %get-tuple-element.186) | copy-start | bytes 1572868
  224.4 61.8 %copy-start.69 = (f32[128]{0:T(128)}, f32[128]{0:T(128)S(1)}, u32[]{:S(2)}) copy-start(f32[128]{0:T(128)S(1)} %broadcast_multiply_fusion.15) | copy-start | bytes 1540
  224.6 61.6 %copy-start.81 = (f32[128]{0:T(128)}, f32[128]{0:T(128)S(1)}, u32[]{:S(2)}) copy-start(f32[128]{0:T(128)S(1)} %add_rsqrt_fusion.3) | copy-start | bytes 1540
  224.6 10.7 %slice-start = ((s8[8388608]{0:T(1024)(128)(4,1)}), s8[4194304]{0:T(1024)(128)(4,1)S(1)}, s32[]{:S(2)}) async-start(s8[8388608]{0:T(1024)(128)(4,1)} %bitcast.440), calls=%async_computation.15 | async-start | bytes 8388608
  225.6 9.7 %copy-start.28 = (bf16[128,1024]{1,0:T(8,128)(2,1)}, bf16[128,1024]{1,0:T(8,128)(2,1)S(1)}, u32[]{:S(2)}) copy-start(bf16[128,1024]{1,0:T(8,128)(2,1)S(1)} %get-tuple-element.120) | copy-start | bytes 786436
  225.6 9.8 %slice-start.1 = ((s8[8388608]{0:T(1024)(128)(4,1)}), s8[4194304]{0:T(1024)(128)(4,1)S(1)}, s32[]{:S(2)}) async-start(s8[8388608]{0:T(1024)(128)(4,1)} %bitcast.440), calls=%async_computation.16 | async-start | bytes 8388608
  236.8 9.4 %copy-start.18 = (bf16[2,1,128,1024]{3,2,1,0:T(8,128)(2,1)S(1)}, bf16[2,1,128,1024]{3,2,1,0:T(8,128)(2,1)}, u32[]{:S(2)}) copy-start(bf16[2,1,128,1024]{3,2,1,0:T(8,128)(2,1)} %param.15) | copy-start | bytes 1572868
  237.1 9.9 %copy-start.73 = (f32[128]{0:T(128)}, f32[128]{0:T(128)S(1)}, u32[]{:S(2)}) copy-start(f32[128]{0:T(128)S(1)} %add_rsqrt_fusion.2) | copy-start | bytes 1540
  237.1 9.9 %copy-start.38 = (bf16[128,3072]{1,0:T(8,128)(2,1)S(1)}, bf16[128,3072]{1,0:T(8,128)(2,1)}, u32[]{:S(2)}) copy-start(bf16[128,3072]{1,0:T(8,128)(2,1)} %copy-done.37) | copy-start | bytes 2359300
  237.1 9.9 %copy-start.39 = (bf16[128,3072]{1,0:T(8,128)(2,1)S(1)}, bf16[128,3072]{1,0:T(8,128)(2,1)}, u32[]{:S(2)}) copy-start(bf16[128,3072]{1,0:T(8,128)(2,1)} %fusion.13) | copy-start | bytes 2359300
  238.1 8.1 collective-permute-start.1
  247.0 11.6 %copy-start.15 = (bf16[128,1024]{1,0:T(8,128)(2,1)}, bf16[128,1024]{1,0:T(8,128)(2,1)S(1)}, u32[]{:S(2)}) copy-start(bf16[128,1024]{1,0:T(8,128)(2,1)S(1)} %get-tuple-element.118) | copy-start | bytes 786436
  258.6 13.5 %slice-start.2 = ((s8[8388608]{0:T(1024)(128)(4,1)}), s8[4194304]{0:T(1024)(128)(4,1)S(1)}, s32[]{:S(2)}) async-start(s8[8388608]{0:T(1024)(128)(4,1)} %bitcast.442), calls=%async_computation.17 | async-start | bytes 8388608
  260.9 11.2 %copy-start.4 = (f32[128,1024]{1,0:T(8,128)}, f32[128,1024]{1,0:T(8,128)S(1)}, u32[]{:S(2)}) copy-start(f32[128,1024]{1,0:T(8,128)S(1)} %get-tuple-element.193) | copy-start | bytes 1572868
  260.9 11.2 %copy-start.71 = (f32[128]{0:T(128)}, f32[128]{0:T(128)S(1)}, u32[]{:S(2)}) copy-start(f32[128]{0:T(128)S(1)} %broadcast_multiply_fusion.13) | copy-start | bytes 1540
  261.6 64.3 %copy-start.67 = (f32[128]{0:T(128)}, f32[128]{0:T(128)S(1)}, u32[]{:S(2)}) copy-start(f32[128]{0:T(128)S(1)} %get-tuple-element.168) | copy-start | bytes 1540
  262.6 9.4 %copy-start.30 = (bf16[128,1024]{1,0:T(8,128)(2,1)}, bf16[128,1024]{1,0:T(8,128)(2,1)S(1)}, u32[]{:S(2)}) copy-start(bf16[128,1024]{1,0:T(8,128)(2,1)S(1)} %get-tuple-element.122) | copy-start | bytes 786436
  262.6 9.5 %slice-start.3 = ((s8[8388608]{0:T(1024)(128)(4,1)}), s8[4194304]{0:T(1024)(128)(4,1)S(1)}, s32[]{:S(2)}) async-start(s8[8388608]{0:T(1024)(128)(4,1)} %bitcast.442), calls=%async_computation.18 | async-start | bytes 8388608
  272.1 14.0 %slice-start.4 = ((s8[16777216]{0:T(1024)(128)(4,1)}), s8[4194304]{0:T(1024)(128)(4,1)S(1)}, s32[]{:S(2)}) async-start(s8[16777216]{0:T(1024)(128)(4,1)} %bitcast.471), calls=%async_computation.19 | async-start | bytes 8388608
  274.0 12.2 %copy-start.2 = (f32[128,1024]{1,0:T(8,128)S(1)}, f32[128,1024]{1,0:T(8,128)}, u32[]{:S(2)}) copy-start(f32[128,1024]{1,0:T(8,128)} %copy-done.1) | copy-start | bytes 1572868
  274.0 12.2 %slice-start.5 = ((s8[16777216]{0:T(1024)(128)(4,1)}), s8[4194304]{0:T(1024)(128)(4,1)S(1)}, s32[]{:S(2)}) async-start(s8[16777216]{0:T(1024)(128)(4,1)} %bitcast.471), calls=%async_computation.20 | async-start | bytes 8388608
  274.0 12.2 %slice-start.6 = ((s8[16777216]{0:T(1024)(128)(4,1)}), s8[4194304]{0:T(1024)(128)(4,1)S(1)}, s32[]{:S(2)}) async-start(s8[16777216]{0:T(1024)(128)(4,1)} %bitcast.471), calls=%async_computation.21 | async-start | bytes 8388608
  274.0 12.2 %slice-start.7 = ((s8[16777216]{0:T(1024)(128)(4,1)}), s8[4194304]{0:T(1024)(128)(4,1)S(1)}, s32[]{:S(2)}) async-start(s8[16777216]{0:T(1024)(128)(4,1)} %bitcast.471), calls=%async_computation.22 | async-start | bytes 8388608
  304.7 7.7 copy-start.87
  304.7 7.7 copy-start.89
  304.7 7.7 collective-permute-start.2
  307.3 18.6 %slice-start.8 = ((s8[16777216]{0:T(1024)(128)(4,1)}), s8[4194304]{0:T(1024)(128)(4,1)S(1)}, s32[]{:S(2)}) async-start(s8[16777216]{0:T(1024)(128)(4,1)} %bitcast.473), calls=%async_computation.23 | async-start | bytes 8388608
  315.0 10.9 %copy-start.51 = (bf16[128,1024]{1,0:T(8,128)(2,1)}, bf16[128,1024]{1,0:T(8,128)(2,1)S(1)}, u32[]{:S(2)}) copy-start(bf16[128,1024]{1,0:T(8,128)(2,1)S(1)} %get-tuple-element.84) | copy-start | bytes 786436
  315.0 10.9 %copy-start.5 = (f32[128,1024]{1,0:T(8,128)S(1)}, f32[128,1024]{1,0:T(8,128)}, u32[]{:S(2)}) copy-start(f32[128,1024]{1,0:T(8,128)} %copy-done.4) | copy-start | bytes 1572868
  315.1 10.9 %slice-start.9 = ((s8[16777216]{0:T(1024)(128)(4,1)}), s8[4194304]{0:T(1024)(128)(4,1)S(1)}, s32[]{:S(2)}) async-start(s8[16777216]{0:T(1024)(128)(4,1)} %bitcast.473), calls=%async_computation.24 | async-start | bytes 8388608
  315.1 10.9 %slice-start.10 = ((s8[16777216]{0:T(1024)(128)(4,1)}), s8[4194304]{0:T(1024)(128)(4,1)S(1)}, s32[]{:S(2)}) async-start(s8[16777216]{0:T(1024)(128)(4,1)} %bitcast.473), calls=%async_computation.25 | async-start | bytes 8388608
  315.1 10.9 %slice-start.11 = ((s8[16777216]{0:T(1024)(128)(4,1)}), s8[4194304]{0:T(1024)(128)(4,1)S(1)}, s32[]{:S(2)}) async-start(s8[16777216]{0:T(1024)(128)(4,1)} %bitcast.473), calls=%async_computation.26 | async-start | bytes 8388608
  315.1 10.9 %copy-start.72 = (f32[128]{0:T(128)S(1)}, f32[128]{0:T(128)}, u32[]{:S(2)}) copy-start(f32[128]{0:T(128)} %copy-done.71) | copy-start | bytes 1540
  340.4 7.3 copy-start.14
  340.4 7.3 copy-start.74
  340.5 7.2 collective-permute-start.3
  348.1 7.9 copy-start.20
  348.1 7.9 copy-start.90
  356.1 201.5 %reduce-scatter.12.cloned.1.call-start = ((), (), s32[]{:S(2)}) async-start(), calls=%async_computation.7 | async-start | bytes 17825792 | tf_op jit(solution)/shard_map/reduce_scatter | solution.py:34
  359.7 11.5 %copy-start.3 = (f32[128,1024]{1,0:T(8,128)S(1)}, f32[128,1024]{1,0:T(8,128)}, u32[]{:S(2)}) copy-start(f32[128,1024]{1,0:T(8,128)} %copy-done.1) | copy-start | bytes 1572868
  359.7 11.5 %copy-start.6 = (f32[128,1024]{1,0:T(8,128)S(1)}, f32[128,1024]{1,0:T(8,128)}, u32[]{:S(2)}) copy-start(f32[128,1024]{1,0:T(8,128)} %copy-done.4) | copy-start | bytes 1572868
  359.7 11.5 %copy-start.68 = (f32[128]{0:T(128)S(1)}, f32[128]{0:T(128)}, u32[]{:S(2)}) copy-start(f32[128]{0:T(128)} %copy-done.67) | copy-start | bytes 1540
  359.7 11.5 %copy-start.70 = (f32[128]{0:T(128)S(1)}, f32[128]{0:T(128)}, u32[]{:S(2)}) copy-start(f32[128]{0:T(128)} %copy-done.69) | copy-start | bytes 1540
  359.7 11.5 %copy-start.82 = (f32[128]{0:T(128)S(1)}, f32[128]{0:T(128)}, u32[]{:S(2)}) copy-start(f32[128]{0:T(128)} %copy-done.81) | copy-start | bytes 1540
  412.2 219.3 %reduce-scatter.16.cloned.1.call-start = ((), (), s32[]{:S(2)}) async-start(), calls=%async_computation.12 | async-start | bytes 278528
  413.4 294.4 %reduce-scatter.18.cloned.1.call-start = ((), (), s32[]{:S(2)}) async-start(), calls=%async_computation.13 | async-start | bytes 1114112
  413.5 146.0 %copy-start.24 = (bf16[128,1024]{1,0:T(8,128)(2,1)S(1)}, bf16[128,1024]{1,0:T(8,128)(2,1)}, u32[]{:S(2)}) copy-start(bf16[128,1024]{1,0:T(8,128)(2,1)} %copy-done.23) | copy-start | bytes 786436
  413.5 146.0 %copy-start.63 = (f32[1,1024]{1,0:T(1,128)S(1)}, f32[1,1024]{1,0:T(1,128)}, u32[]{:S(2)}) copy-start(f32[1,1024]{1,0:T(1,128)} %copy-done.62) | copy-start | bytes 12292
  415.2 367.1 %reduce-scatter.20.cloned.1.call-start = ((), (), s32[]{:S(2)}) async-start(), calls=%async_computation.14 | async-start | bytes 278528
  416.3 404.8 %all-gather.38.cloned.1.call-start = ((), (), s32[]{:S(2)}) async-start(), calls=%async_computation.11 | async-start | bytes 2621440 | tf_op jit(solution)/shard_map/all_gather | solution.py:39
  443.4 117.2 %copy-start.27 = (bf16[1,128,1024]{2,1,0:T(8,128)(2,1)S(1)}, bf16[1,128,1024]{2,1,0:T(8,128)(2,1)}, u32[]{:S(2)}) copy-start(bf16[1,128,1024]{2,1,0:T(8,128)(2,1)} %get-tuple-element.135) | copy-start | bytes 786436
  443.4 396.2 %all-gather.34.cloned.1.call-start = ((), (), s32[]{:S(2)}) async-start(), calls=%async_computation.9 | async-start | bytes 1966080 | tf_op jit(solution)/shard_map/all_gather | solution.py:39
  559.5 308.5 %all-gather.36.cloned.1.call-start = ((), (), s32[]{:S(2)}) async-start(), calls=%async_computation.10 | async-start | bytes 2621440 | tf_op jit(solution)/shard_map/all_gather | solution.py:39
  567.4 256.9 %slice-start.12 = ((bf16[1,64,8192]{2,1,0:T(8,128)(2,1)}), bf16[1,64,1024]{2,1,0:T(8,128)(2,1)S(1)}, s32[]{:S(2)}) async-start(bf16[1,64,8192]{2,1,0:T(8,128)(2,1)} %reduce-scatter.12.cloned.1.call-done), calls=%async_computation.27 | async-start | bytes 262144 | tf_op jit(solution)/shard_map/split | solution.py:34
  (67 other events, 203.6 us)
Sparse Core Ops, SparseCore 0:
  10.8 114.9 all-gather.29
  127.9 70.4 all-gather.31
  356.2 87.1 reduce-scatter.13
  446.7 110.8 reduce-scatter.11
  561.1 70.2 reduce-scatter.15
  635.4 72.3 reduce-scatter.17
  711.0 71.1 reduce-scatter.19
  784.0 27.8 all-gather.37
  813.7 25.9 all-gather.33
  841.9 26.0 all-gather.35
where the time goes:
time: 886 us; the launch traced here: 878 us
  waiting for transfers between devices  479 us (54%)
  matrix products  163 us (18%)
  blocking collectives  134 us (15%)
  other arithmetic  45.4 us (5%)
  local copies, waits for them, and re-layouts  28.5 us (3%)
  between operations  16.6 us (2%)
  starting transfers between devices  10.9 us (1%)
    unnamed x13, waiting for transfers between devices  181 us
    reduce_scatter x1, waiting for transfers between devices, in_one_piece(): lax.psum_scatter(both, axis, scatter_dimension=dim, tiled=True)  114 us
    all_gather x10, blocking collectives, total_of_pieces(): return lax.all_gather(shard, axis).astype(jnp.float32).sum(0)  77.2 us
    dot_general x12, matrix products, matmul_back(): lax.dot_general(left, right, (((1,), (1,)), ((), ())), preferred_element_...  70.3 us
    all_gather x1, waiting for transfers between devices, side_by_side(): whole = lax.all_gather(both, axis, axis=dim, tiled=True)  57.8 us
    dot_general x12, matrix products, matmul(): return jnp.dot(left, right, preferred_element_type=jnp.float32)  56.7 us
    all_gather x1, waiting for transfers between devices, on_device(): lax.all_gather(down_weight, 'shard', axis=1, tiled=True)  56 us
    all_gather x2, blocking collectives, side_by_side(): whole = lax.all_gather(both, axis, axis=dim, tiled=True)  38.3 us
  transfers between devices with their start and end apart: 14, of which 13 were waited for; matrix products, arithmetic and copies ran while one was open for 12% of the time, Pallas kernels for 0%

commit v1 on v0

v1 whole, which is shorter than its diff:
```python
import jax
import jax.numpy as jnp
from jax import lax
from jax.sharding import Mesh
from jax.sharding import PartitionSpec as P

HEADS = 16
HEAD_DIM = 64
LEN = 128
WIDTH = 1024
HIDDEN = 4096
SCALE = HEAD_DIM ** (-0.5)
EPSILON = 1e-06

F32 = jnp.float32
BF16 = jnp.bfloat16


def matmul(left, right):
    return jnp.dot(left, right, preferred_element_type=F32)


def matmul_back(left, right):
    return lax.dot_general(left, right, (((1,), (1,)), ((), ())), preferred_element_type=F32)


def matmul_rows(left, right):
    return lax.dot_general(left, right, (((0,), (0,)), ((), ())), preferred_element_type=F32)


def gelu_exact(values):
    return jax.nn.gelu(values, approximate=False)


def swap_cores(value):
    return lax.ppermute(value, "core", [(0, 1), (1, 0)])


def swap_far(value):
    return lax.ppermute(value, "far", [(0, 1), (1, 0)])


def norm_forward(totals, gain_row, shift_row):
    average = jnp.mean(totals, -1, keepdims=True)
    centred = totals - average
    inverse = lax.rsqrt(jnp.mean(centred * centred, -1, keepdims=True) + EPSILON)
    normed = centred * inverse
    return (normed * gain_row + shift_row, normed, inverse)


def norm_backward(upstream, normed, inverse, gain_row):
    scaled = upstream * gain_row
    return inverse * (
        scaled
        - jnp.mean(scaled, -1, keepdims=True)
        - normed * jnp.mean(scaled * normed, -1, keepdims=True)
    )


def gather_weights(project, output, upward, downward, vectors):
    core = lax.axis_index("core")
    half = lax.dynamic_slice_in_dim(
        jnp.concatenate([project, output, upward], 1), core * 32, 32, 0
    )
    down = lax.dynamic_slice_in_dim(downward, core * 128, 128, 0)
    down = down.reshape(4, 32, WIDTH).transpose(1, 0, 2).reshape(32, HIDDEN)
    flat = jnp.concatenate(vectors).reshape(6, 128)
    extra = jnp.concatenate([flat, jnp.zeros((26, 128), BF16)], 0)
    packed = jnp.concatenate([half, down, extra], 1)
    whole = lax.all_gather(packed, ("z", "y", "core"), axis=0, tiled=True)
    rows = whole[:, 12288:].reshape(16, 64, 128)[:, :6].astype(F32)
    pairs = rows[:, :4].reshape(16, 8, 64).transpose(1, 0, 2).reshape(8, WIDTH)
    ups = rows[:, 4:].reshape(HIDDEN)
    down_whole = (
        whole[:, 8192:12288]
        .reshape(32, 32, 4, WIDTH)
        .transpose(0, 2, 1, 3)
        .reshape(HIDDEN, WIDTH)
    )
    return (
        (whole[:, :3072], whole[:, 3072:4096], whole[:, 4096:8192], down_whole),
        (pairs, ups),
    )


def layer_forward(rows16, weights, vectors):
    project, output, upward, downward = weights
    pairs, ups = vectors
    query_row, value_row, output_row, down_row, gain_one, shift_one, gain_two, shift_two = pairs
    biases = jnp.concatenate([query_row, jnp.zeros((WIDTH,), F32), value_row])
    packed = (matmul(rows16, project) + biases).astype(BF16)
    heads_view = packed.reshape(-1, LEN, 3, HEADS, HEAD_DIM)
    scores = (
        jnp.einsum(
            "sqhe,skhe->shqk", heads_view[:, :, 0], heads_view[:, :, 1], preferred_element_type=F32
        )
        * SCALE
    )
    log_totals = jax.nn.logsumexp(scores, axis=-1, keepdims=True)
    soft16 = jnp.exp(scores - log_totals).astype(BF16)
    attended = (
        jnp.einsum("shqk,skhe->sqhe", soft16, heads_view[:, :, 2], preferred_element_type=F32)
        .reshape(-1, WIDTH)
        .astype(BF16)
    )
    residual_one = rows16.astype(F32) + (matmul(attended, output) + output_row)
    hidden, normed_one, inverse_one = norm_forward(residual_one, gain_one, shift_one)
    hidden16 = hidden.astype(BF16)
    upper = matmul(hidden16, upward) + ups
    active16 = gelu_exact(upper).astype(BF16)
    residual_two = hidden + (matmul(active16, downward) + down_row)
    result, normed_two, inverse_two = norm_forward(residual_two, gain_two, shift_two)
    kept = (
        rows16,
        packed,
        log_totals,
        attended,
        normed_one,
        inverse_one,
        hidden16,
        upper,
        active16,
        normed_two,
        inverse_two,
    )
    return (result.astype(BF16), kept)


def layer_backward(upstream, kept, weights, vectors):
    project, output, upward, downward = weights
    pairs, ups = vectors
    query_row, value_row, output_row, down_row, gain_one, shift_one, gain_two, shift_two = pairs
    (
        rows16,
        packed,
        log_totals,
        attended,
        normed_one,
        inverse_one,
        hidden16,
        upper,
        active16,
        normed_two,
        inverse_two,
    ) = kept
    upstream = upstream.astype(F32)
    gain_two_grad = jnp.sum(upstream * normed_two, 0)
    shift_two_grad = jnp.sum(upstream, 0)
    total_two_grad = norm_backward(upstream, normed_two, inverse_two, gain_two)
    down_grad16 = total_two_grad.astype(BF16)
    active_grad = matmul_back(down_grad16, downward)
    upper_grad16 = jax.vjp(gelu_exact, upper)[1](active_grad)[0].astype(BF16)
    hidden_grad = matmul_back(upper_grad16, upward) + total_two_grad
    gain_one_grad = jnp.sum(hidden_grad * normed_one, 0)
    shift_one_grad = jnp.sum(hidden_grad, 0)
    total_grad = norm_backward(hidden_grad, normed_one, inverse_one, gain_one)
    branch_grad16 = total_grad.astype(BF16)
    attended_grad16 = (
        matmul_back(branch_grad16, output).astype(BF16).reshape(-1, LEN, HEADS, HEAD_DIM)
    )
    heads_view = packed.reshape(-1, LEN, 3, HEADS, HEAD_DIM)
    queries = heads_view[:, :, 0]
    keys_all = heads_view[:, :, 1]
    values_all = heads_view[:, :, 2]
    scores = jnp.einsum("sqhe,skhe->shqk", queries, keys_all, preferred_element_type=F32) * SCALE
    soft = jnp.exp(scores - log_totals)
    soft16 = soft.astype(BF16)
    values_grad = jnp.einsum(
        "shqk,sqhe->skhe", soft16, attended_grad16, preferred_element_type=F32
    )
    soft_grad = jnp.einsum(
        "sqhe,skhe->shqk", attended_grad16, values_all, preferred_element_type=F32
    )
    scores_grad16 = (
        soft * (soft_grad - jnp.sum(soft_grad * soft, -1, keepdims=True))
    ).astype(BF16)
    queries_grad = (
        jnp.einsum("shqk,skhe->sqhe", scores_grad16, keys_all, preferred_element_type=F32) * SCALE
    )
    keys_grad = (
        jnp.einsum("shqk,sqhe->skhe", scores_grad16, queries, preferred_element_type=F32) * SCALE
    )
    packed_grad16 = (
        jnp.stack([queries_grad, keys_grad, values_grad], 2).reshape(-1, 3 * WIDTH).astype(BF16)
    )
    rows_grad = matmul_back(packed_grad16, project) + total_grad
    packed_sums = jnp.sum(packed_grad16.astype(F32), 0)
    vector_grads = (
        jnp.stack(
            [
                packed_sums[:WIDTH],
                packed_sums[2 * WIDTH :],
                jnp.sum(branch_grad16.astype(F32), 0),
                jnp.sum(down_grad16.astype(F32), 0),
                gain_one_grad,
                shift_one_grad,
                gain_two_grad,
                shift_two_grad,
            ]
        ),
        jnp.sum(upper_grad16.astype(F32), 0),
    )
    pieces = (
        (rows16, packed_grad16),
        (attended, branch_grad16),
        (hidden16, upper_grad16),
        (active16, down_grad16),
    )
    return (rows_grad.astype(BF16), pieces, vector_grads)


def reduce_grads(pieces, vector_grads):
    core = lax.axis_index("core")

    def half(array, which):
        width = array.shape[1] // 2
        return lax.dynamic_slice_in_dim(array, which * width, width, 1)

    def block(left, right, which):
        return matmul_rows(left, half(right, which))

    others = [swap_cores(block(left, right, 1 - core).astype(BF16)) for left, right in pieces]
    sums = [
        (block(left, right, core) + other.astype(F32)).astype(BF16)
        for (left, right), other in zip(pieces, others)
    ]
    project, output, upward, downward = sums
    parts = [
        *(project.reshape(16, 64, 3, 512)[:, :, k] for k in range(3)),
        output.reshape(16, 64, 512),
        *(upward.reshape(16, 64, 4, 512)[:, :, k] for k in range(4)),
        downward.reshape(16, 256, 512),
    ]
    pairs, ups = vector_grads
    first = pairs.reshape(8, 16, 64).transpose(1, 0, 2).reshape(16, 1, 512)
    second = jnp.concatenate([ups.reshape(16, 1, 256), jnp.zeros((16, 1, 256), F32)], 2)
    extra = jnp.concatenate([first, second, jnp.zeros((16, 14, 512), F32)], 1).astype(BF16)
    packed = jnp.concatenate([*parts, extra], 1).reshape(16 * 784, 512)
    owned = lax.psum_scatter(packed, ("z", "y"), scatter_dimension=0, tiled=True)
    owned = lax.optimization_barrier(owned)
    total = owned.astype(F32) + swap_far(owned).astype(F32)
    total = lax.optimization_barrier(total)
    other = swap_cores(total)
    low = jnp.where(core == 0, total, other)
    high = jnp.where(core == 0, other, total)

    def columns(start, count, rows=64):
        left = [low[start + k * rows : start + (k + 1) * rows] for k in range(count)]
        right = [high[start + k * rows : start + (k + 1) * rows] for k in range(count)]
        return jnp.concatenate(left + right, 1)[None]

    vectors = (total[768:770] + other[768:770]).reshape(1024)
    narrow = [vectors[64 * k : 64 * (k + 1)][None] for k in range(8)]
    query, value, output_b, down_b, gain_one, shift_one, gain_two, shift_two = narrow
    return (
        columns(0, 3),
        columns(192, 1),
        columns(256, 4),
        columns(512, 1, 256),
        query,
        value,
        output_b,
        vectors[512:768][None],
        down_b,
        gain_one,
        shift_one,
        gain_two,
        shift_two,
    )


def on_device(
    layer_input,
    cotangent,
    project_weight,
    output_weight,
    up_weight,
    down_weight,
    query_bias,
    value_bias,
    output_bias,
    up_bias,
    down_bias,
    first_gain,
    first_shift,
    second_gain,
    second_shift,
):
    first_section = lax.axis_index("section") == 0
    weights, vectors = gather_weights(
        project_weight[0],
        output_weight[0],
        up_weight[0],
        down_weight[0],
        (
            query_bias[0],
            value_bias[0],
            output_bias[0],
            down_bias[0],
            first_gain[0],
            first_shift[0],
            second_gain[0],
            second_shift[0],
            up_bias[0],
        ),
    )
    shape = layer_input.shape
    own_rows = layer_input.reshape(-1, WIDTH)
    own_grad = cotangent.reshape(-1, WIDTH)

    early, _ = layer_forward(own_rows, weights, vectors)
    received = lax.ppermute(early, "section", [(0, 1)])
    rows16 = jnp.where(first_section, own_rows, received)
    result, kept = layer_forward(rows16, weights, vectors)

    early_grad, _, _ = layer_backward(own_grad, kept, weights, vectors)
    back = lax.ppermute(early_grad, "section", [(1, 0)])
    upstream = jnp.where(first_section, back, own_grad)
    rows_grad, pieces, vector_grads = layer_backward(upstream, kept, weights, vectors)
    return (
        result.reshape(1, *shape),
        rows_grad.reshape(1, *shape),
        *reduce_grads(pieces, vector_grads),
    )


def solution(mesh):
    devices = mesh.devices.reshape(2, 2, 2, 4, 4)
    fine = Mesh(devices, ("section", "far", "core", "z", "y"))
    shard = ("z", "y")
    seqs = P(None, ("far", "core", "z", "y"), None, None)
    matrix = P("section", shard, None)
    vector = P("section", shard)
    rows = P("section", None, ("far", "core", "z", "y"), None, None)
    return jax.shard_map(
        on_device,
        mesh=fine,
        in_specs=(seqs, seqs, *([matrix] * 4), *([vector] * 9)),
        out_specs=(rows, rows, *([matrix] * 4), *([vector] * 9)),
        check_vma=False,
    )
```

time: 886 us -> 630 us (0.71)
  waiting for transfers between devices: 479 us -> 233 us
  local copies, waits for them, and re-layouts: 28.5 us -> 187 us
  blocking collectives: 134 us -> 0 us
  other arithmetic: 45.4 us -> 21.6 us
  matrix products: 163 us -> 152 us
    unnamed x13 -> x2, waiting for transfers between devices: 181 us -> 0.03 us
    all_gather x13 -> x0, blocking collectives: 134 us -> none  [the longest x10 77.2 us: total_of_pieces(): return lax.all_gather(shard, axis).astype(jnp.float32).sum(0)]
    concatenate x2 -> x4, local copies, waits for them, and re-layouts: 0.08 us -> 66.5 us  [the longest x1 61 us: reduce_grads(): packed = jnp.concatenate([*parts, extra], 1).reshape(16 * 784, 512)]
    reshape x0 -> x13, local copies, waits for them, and re-layouts: none -> 49 us  [the longest x1 14.7 us: gather_weights(): down_whole = whole[:, 8192:12288].reshape(32, 32, 4, WIDTH).transpose(0,...]
    reduce_scatter x2 -> x1, waiting for transfers between devices: 141 us -> 93.9 us  [reduce_grads(): lax.psum_scatter(packed, ('z', 'y'), scatter_dimension=0, tiled=True)]
    all_gather x5 -> x1, waiting for transfers between devices: 142 us -> 96.6 us  [gather_weights(): whole = lax.all_gather(packed, ('z', 'y', 'core'), axis=0, tiled=True)]
    slice x0 -> x11, local copies, waits for them, and re-layouts: none -> 37.7 us  [the longest x1 13.4 us: reduce_grads(): upward.reshape(16, 64, 4, 512)[:, :, k]]
    ppermute x4 -> x8, waiting for transfers between devices: 14.9 us -> 42 us  [the longest x1 17.4 us: swap_far(): return lax.ppermute(value, 'far', [(0, 1), (1, 0)])]
  transfers between devices with their start and end apart: 14 -> 10, of which waited for: 13 -> 6; matrix products, arithmetic and copies ran while one was open for 12% -> 13% of each run, Pallas kernels for 0% -> 0%
where the time goes in v1:
time: 630 us; the launch traced here: 620 us
  waiting for transfers between devices  233 us (37%)
  local copies, waits for them, and re-layouts  187 us (30%)
  matrix products  152 us (24%)
  other arithmetic  21.6 us (3%)
  between operations  15.3 us (2%)
  starting transfers between devices  12 us (2%)
    all_gather x1, waiting for transfers between devices, gather_weights(): whole = lax.all_gather(packed, ('z', 'y', 'core'), axis=0, tiled=True)  96.6 us
    reduce_scatter x1, waiting for transfers between devices, reduce_grads(): lax.psum_scatter(packed, ('z', 'y'), scatter_dimension=0, tiled=True)  93.9 us
    concatenate x1, local copies, waits for them, and re-layouts, reduce_grads(): packed = jnp.concatenate([*parts, extra], 1).reshape(16 * 784, 512)  61 us
    dot_general x7, matrix products, matmul(): return jnp.dot(left, right, preferred_element_type=F32)  53.3 us
    dot_general x7, matrix products, matmul_back(): lax.dot_general(left, right, (((1,), (1,)), ((), ())), preferred_element_...  53 us
    dot_general x8, matrix products, matmul_rows(): lax.dot_general(left, right, (((0,), (0,)), ((), ())), preferred_element_...  33.3 us
    ppermute x1, waiting for transfers between devices, swap_far(): return lax.ppermute(value, 'far', [(0, 1), (1, 0)])  17.4 us
    unnamed x102, local copies, waits for them, and re-layouts  17.2 us
  transfers between devices with their start and end apart: 10, of which 6 were waited for; matrix products, arithmetic and copies ran while one was open for 13% of the time, Pallas kernels for 0%

profile of v1, /device:TPU:1, one launch (start us, length us, event | category | flops | bytes accessed | tf_op | source)
XLA Modules:
  0.0 620.0 jit_solution(6786276186079728358)
XLA Ops:
  10.1 5.4 concatenate.40
  16.5 96.6 %all-gather.2.cloned.1.call-done = bf16[1024,12416]{1,0:T(8,128)(2,1)} async-done(((bf16[32,12416]{1,0:T(8,128)(2,1)}), bf16[1024,12416]{1,0:T(8,128)(2,1)}) %all-gather.2.cloned.1.call-update) | async-done | bytes 25427984 | tf_op jit(solution)/shard_map/all_gather | solution.py:70
  114.6 6.1 fusion.50
  120.7 2.4 reshape.298
  126.4 2.4 fusion.282
  129.3 7.7 %slice.236 = bf16[1024,4096]{1,0:T(8,128)(2,1)} slice(bf16[1024,12416]{1,0:T(8,128)(2,1)} %all-gather.2.cloned.1.call-done), slice={[0:1024], [8192:12288]} | slice | bytes 16777216 | tf_op jit(solution)/shard_map/slice | solution.py:75
  137.0 14.7 %reshape.299 = bf16[32,32,4,1024]{3,2,1,0:T(4,128)(2,1)} reshape(bf16[1024,4096]{1,0:T(8,128)(2,1)} %slice.236) | data formatting | bytes 16777216 | tf_op jit(solution)/shard_map/reshape | solution.py:76
  151.7 10.3 %copy.90 = bf16[32,4,32,1024]{3,2,1,0:T(8,128)(2,1)} copy(bf16[32,4,32,1024]{3,1,2,0:T(4,128)(2,1)} %bitcast.233) | data formatting | bytes 16777216 | tf_op jit(solution)/shard_map/transpose | solution.py:77
  162.0 19.0 %fusion.283 = (f32[256]{0:T(256)S(1)}, f32[256,1024]{1,0:T(8,128)S(1)}) fusion(f32[1024]{0:T(1024)S(1)} %add.235, bf16[4096,1024]{1,0:T(8,128)(2,1)} %bitcast.235, f32[4096]{0:T(1024)S(1)} %bitcast.273, bf16[1024,12416]{1,0:T(8,128)(2,1)} %all-gather.2.cloned.1.call-done, f32[256,1024]{1,0:T(8,128)S(1)} %get-tuple-element.130, f32[1024]{0:T(1024)S(1)} %add.229, ...), kind=kOutput, calls=%fused_computation.374 | convolution fusion | flops 4367319040 | bytes 19964928 | tf_op jit(solution)/shard_map/dot_general | solution.py:20
  181.7 3.1 collective-permute-start
  185.0 10.8 %collective-permute-done = bf16[256,1024]{1,0:T(8,128)(2,1)S(1)} collective-permute-done((bf16[256,1024]{1,0:T(8,128)(2,1)S(1)}, bf16[256,1024]{1,0:T(8,128)(2,1)S(1)}, u32[]{:S(2)}, u32[]{:S(2)}) %collective-permute-start) | collective-permute-done | bytes 524320 | tf_op jit(solution)/shard_map/ppermute | solution.py:312
  196.7 4.6 fusion.44
  201.3 3.3 reshape.316
  204.6 3.4 fusion.280
  208.9 1.6 copy.141
  210.5 1.5 multiply_reduce_fusion.2
  212.5 1.3 fusion.171
  213.8 2.0 copy.142
  215.8 1.6 fusion.145
  218.0 2.7 fusion.288
  221.1 16.0 %multiply_convert_fusion = (bf16[256,4096]{1,0:T(8,128)(2,1)S(1)}, f32[256,4096]{1,0:T(8,128)}, f32[256,4096]{1,0:T(8,128)}) fusion(f32[4096]{0:T(1024)S(1)} %bitcast.274, bf16[1024,12416]{1,0:T(8,128)(2,1)} %all-gather.2.cloned.1.call-done, f32[1024]{0:T(1024)S(1)} %add.229, f32[1024]{0:T(1024)S(1)} %mul.313, f32[256]{0:T(256)S(1)} %add_rsqrt_fusion.1, ...), kind=kOutput, calls=%fused_computation.22 | convolution fusion | flops 2218000384 | bytes 19949568 | tf_op jit(solution)/shard_map/dot_general | solution.py:20
  237.1 2.5 fusion.289
  240.5 1.3 subtract_multiply_fusion.2
  241.8 16.4 %fusion.269 = (f32[256]{0:T(256)S(1)}, f32[256]{0:T(256)S(1)}, f32[256,1024]{1,0:T(8,128)}) fusion(f32[256]{0:T(256)S(1)} %add_rsqrt_fusion.1, f32[256,1024]{1,0:T(8,128)} %copy-done.2, f32[256]{0:T(256)S(1)} %broadcast_multiply_fusion.8, f32[1024]{0:T(1024)S(1)} %mul.313, f32[256,1024]{1,0:T(8,128)} %subtract_multiply_fusion.2, ...), kind=kOutput, calls=%fused_computation.363 | convolution fusion | flops 4311744512 | bytes 29368320 | tf_op jit(solution)/shard_map/dot_general | solution.py:24
  258.3 3.9 fusion.130
  262.1 2.5 reshape.317
  264.6 2.8 copy.98
  267.4 1.8 multiply_reduce_fusion.1
  272.1 1.6 copy.103
  273.8 5.6 fusion.139
  279.4 1.3 collective-permute-start.1
  280.7 13.5 %collective-permute-done.1 = bf16[256,1024]{1,0:T(8,128)(2,1)} collective-permute-done((bf16[256,1024]{1,0:T(8,128)(2,1)}, bf16[256,1024]{1,0:T(8,128)(2,1)}, u32[]{:S(2)}, u32[]{:S(2)}) %collective-permute-start.1) | collective-permute-done | bytes 524320 | tf_op jit(solution)/shard_map/ppermute | solution.py:317
  295.5 2.5 fusion.156
  298.0 1.6 fusion.272
  299.6 11.2 %fusion.270 = (bf16[4096]{0:T(1024)(128)(2,1)S(1)}, bf16[256,4096]{1,0:T(8,128)(2,1)S(1)}) fusion(f32[256,4096]{1,0:T(8,128)S(1)} %copy-done.35, f32[256,4096]{1,0:T(8,128)} %get-tuple-element.137, bf16[256,1024]{1,0:T(8,128)(2,1)S(1)} %get-tuple-element.82, bf16[4096,1024]{1,0:T(8,128)(2,1)} %bitcast.237), kind=kOutput, calls=%fused_computation.364 | convolution fusion | flops 2163208192 | bytes 19406848 | tf_op jit(solution)/shard_map/dot_general | solution.py:24
  310.9 6.3 %multiply_reduce_fusion.4 = (bf16[1024]{0:T(1024)(128)(2,1)S(1)}, f32[256]{0:T(256)S(1)}, f32[256]{0:T(256)S(1)}, bf16[1024]{0:T(1024)(128)(2,1)S(1)}, f32[256,1024]{1,0:T(8,128)S(1)}) fusion(f32[256]{0:T(256)S(1)} %add_rsqrt_fusion.1, f32[256,1024]{1,0:T(8,128)S(1)} %copy-done.4, f32[256]{0:T(256)S(1)} %broadcast_multiply_fusion.8, f32[1024]{0:T(1024)S(1)} %mul.313, ...), kind=kOutput, calls=%fused_computation.180 | convolution fusion | flops 2152199680 | bytes 14176256 | tf_op jit(solution)/shard_map/dot_general | solution.py:24
  318.2 3.3 fusion.133
  321.5 2.7 reshape.318
  324.2 2.8 copy.105
  327.0 1.8 multiply_reduce_fusion
  332.1 1.6 copy.110
  334.0 2.8 convolution_convert_fusion.1
  336.7 1.9 collective-permute-start.2
  338.6 4.6 convolution_convert_fusion.2
  343.7 2.5 convolution_convert_fusion.3
  346.8 4.8 convolution_convert_fusion
  352.2 2.9 add_convert_fusion.6
  355.1 4.5 add_convert_fusion.2
  359.6 10.1 %reshape.307 = bf16[16,64,3,512]{3,2,1,0:T(4,128)(2,1)} reshape(bf16[1024,1536]{1,0:T(8,128)(2,1)} %add_convert_fusion.2) | data formatting | bytes 6291456 | tf_op jit(solution)/shard_map/reshape | solution.py:229
  369.7 10.4 %fusion.279 = (bf16[16,64,1,512]{3,2,1,0:T(2,128)(2,1)S(1)}, bf16[16,64,1,512]{3,2,1,0:T(2,128)(2,1)S(1)}, bf16[16,64,1,512]{3,2,1,0:T(2,128)(2,1)S(1)}) fusion(bf16[16,64,3,512]{3,2,1,0:T(4,128)(2,1)} %reshape.307), kind=kLoop, calls=%fused_computation.370 | loop fusion | bytes 6291456 | tf_op jit(solution)/shard_map/slice | solution.py:229
  384.0 5.6 add_convert_fusion.1
  389.5 7.8 %reshape.309 = bf16[16,64,4,512]{3,2,1,0:T(4,128)(2,1)} reshape(bf16[1024,2048]{1,0:T(8,128)(2,1)} %add_convert_fusion.1) | data formatting | bytes 8388608 | tf_op jit(solution)/shard_map/reshape | solution.py:231
  397.4 13.4 %fusion.278 = (bf16[16,64,1,512]{3,2,1,0:T(2,128)(2,1)S(1)}, bf16[16,64,1,512]{3,2,1,0:T(2,128)(2,1)S(1)}, bf16[16,64,1,512]{3,2,1,0:T(2,128)(2,1)S(1)}, bf16[16,64,1,512]{3,2,1,0:T(2,128)(2,1)S(1)}) fusion(bf16[16,64,4,512]{3,2,1,0:T(4,128)(2,1)} %reshape.309), kind=kLoop, calls=%fused_computation.369 | loop fusion | bytes 8388608 | tf_op jit(solution)/shard_map/slice | solution.py:231
  412.0 1.3 copy.203
  414.6 1.3 copy.205
  415.9 5.6 add_convert_fusion
  421.6 61.0 %concatenate.45 = bf16[16,784,512]{2,1,0:T(8,128)(2,1)} concatenate(bf16[16,64,512]{2,1,0:T(8,128)(2,1)} %bitcast.251, bf16[16,64,512]{2,1,0:T(8,128)(2,1)} %bitcast.250, bf16[16,64,512]{2,1,0:T(8,128)(2,1)} %bitcast.249, bf16[16,64,512]{2,1,0:T(8,128)(2,1)S(1)} %bitcast.248, bf16[16,64,512]{2,1,0:T(8,128)(2,1)} %bitcast.255, bf16[16,64,512]{2,1,0:T(8,128)(2,1)} %bitcast.254, ...), dimensions={1} | concatenate | bytes 25690112 | tf_op jit(solution)/shard_map/concatenate | solution.py:238
  482.6 93.9 %reduce-scatter.2.cloned.1.call-done = bf16[784,512]{1,0:T(8,128)(2,1)} async-done(((bf16[12544,512]{1,0:T(8,128)(2,1)}), bf16[784,512]{1,0:T(8,128)(2,1)}) %reduce-scatter.2.cloned.1.call-update) | async-done | bytes 802832 | tf_op jit(solution)/shard_map/reduce_scatter | solution.py:239
  576.5 3.0 collective-permute-start.6
  579.4 17.4 %collective-permute-done.6 = bf16[784,512]{1,0:T(8,128)(2,1)S(1)} collective-permute-done((bf16[784,512]{1,0:T(8,128)(2,1)}, bf16[784,512]{1,0:T(8,128)(2,1)S(1)}, u32[]{:S(2)}, u32[]{:S(2)}) %collective-permute-start.6) | collective-permute-done | bytes 802848 | tf_op jit(solution)/shard_map/ppermute | solution.py:40
  596.9 1.4 convert_add_fusion
  598.2 2.0 collective-permute-start.7
  600.2 6.3 %fusion.136 = bf16[256,1024]{1,0:T(8,128)(2,1)} fusion(bf16[1024,12416]{1,0:T(8,128)(2,1)} %all-gather.2.cloned.1.call-done, bf16[384,8,2,128]{3,2,1,0:T(2,128)(2,1)} %bitcast.242, f32[256]{0:T(256)S(1)} %broadcast_multiply_fusion, f32[256]{0:T(256)S(1)} %broadcast_multiply_fusion.1, f32[256,1024]{1,0:T(8,128)} %copy-done.30, f32[1024]{0:T(1024)S(1)} %mul.313, ...), kind=kOutput, calls=%fused_computation.158 | convolution fusion | flops 1612972032 | bytes 10493952 | tf_op jit(solution)/shard_map/dot_general | solution.py:24
  608.4 1.8 broadcast_select_fusion
  (198 shorter events, 34.9 us)
Async XLA Ops:
  7.2 1.1 copy-start
  7.2 107.4 %copy-start.31 = (bf16[2,1,128,1024]{3,2,1,0:T(8,128)(2,1)S(1)}, bf16[2,1,128,1024]{3,2,1,0:T(8,128)(2,1)}, u32[]{:S(2)}) copy-start(bf16[2,1,128,1024]{3,2,1,0:T(8,128)(2,1)} %param.15) | copy-start | bytes 1572868
  7.2 105.9 %all-gather.2.cloned.1.call-start = ((), (), s32[]{:S(2)}) async-start(), calls=%async_computation.1 | async-start | bytes 26222592 | tf_op jit(solution)/shard_map/all_gather | solution.py:70
  16.5 560.0 %reduce-scatter.2.cloned.1.call-start = ((), (), s32[]{:S(2)}) async-start(), calls=%async_computation.2 | async-start | bytes 13647872 | tf_op jit(solution)/shard_map/reduce_scatter | solution.py:239
  162.0 22.8 %copy-start.12 = (bf16[2,1,128,1024]{3,2,1,0:T(8,128)(2,1)S(1)}, bf16[2,1,128,1024]{3,2,1,0:T(8,128)(2,1)}, u32[]{:S(2)}) copy-start(bf16[2,1,128,1024]{3,2,1,0:T(8,128)(2,1)} %param.16) | copy-start | bytes 1572868
  181.7 14.2 %collective-permute-start = (bf16[256,1024]{1,0:T(8,128)(2,1)S(1)}, bf16[256,1024]{1,0:T(8,128)(2,1)S(1)}, u32[]{:S(2)}, u32[]{:S(2)}) collective-permute-start(bf16[256,1024]{1,0:T(8,128)(2,1)S(1)} %add_convert_fusion.12), channel_id=1, source_target_pairs={{0,64},{1,65},{2,66},{3,67},{4,68},{5,69},{6,70},{7,71},{8,72},{9,... | collective-permute-start | bytes 1572872 | tf_op jit(solution)/shard_map/ppermute | solution.py:312
  195.9 0.8 copy-start.18
  208.9 4.9 copy-start.13
  218.0 3.0 copy-start.23
  218.0 19.0 %slice-start = ((s8[8388608]{0:T(1024)(128)(4,1)}), s8[4194304]{0:T(1024)(128)(4,1)S(1)}, s32[]{:S(2)}) async-start(s8[8388608]{0:T(1024)(128)(4,1)} %bitcast.238), calls=%async_computation.3 | async-start | bytes 8388608
  220.8 16.3 %copy-start.2 = (f32[256,1024]{1,0:T(8,128)}, f32[256,1024]{1,0:T(8,128)S(1)}, u32[]{:S(2)}) copy-start(f32[256,1024]{1,0:T(8,128)S(1)} %get-tuple-element.136) | copy-start | bytes 3145732
  221.1 16.0 %slice-start.1 = ((s8[8388608]{0:T(1024)(128)(4,1)}), s8[4194304]{0:T(1024)(128)(4,1)S(1)}, s32[]{:S(2)}) async-start(s8[8388608]{0:T(1024)(128)(4,1)} %bitcast.238), calls=%async_computation.4 | async-start | bytes 8388608
  237.0 2.5 copy-start.8
  239.5 1.0 copy-start.6
  267.4 2.5 copy-start.14
  269.2 1.1 copy-start.16
  269.2 1.9 copy-start.10
  269.2 1.9 copy-start.22
  271.1 2.7 copy-start.3
  271.1 2.6 copy-start.34
  279.4 14.8 %collective-permute-start.1 = (bf16[256,1024]{1,0:T(8,128)(2,1)}, bf16[256,1024]{1,0:T(8,128)(2,1)}, u32[]{:S(2)}, u32[]{:S(2)}) collective-permute-start(bf16[256,1024]{1,0:T(8,128)(2,1)} %fusion.139), channel_id=1, source_target_pairs={{64,0},{65,1},{66,2},{67,3},{68,4},{69,5},{70,6},{71,7},{72,8},{73... | collective-permute-start | bytes 1572872 | tf_op jit(solution)/shard_map/ppermute | solution.py:317
  280.7 18.9 %copy-start.35 = (f32[256,4096]{1,0:T(8,128)S(1)}, f32[256,4096]{1,0:T(8,128)}, u32[]{:S(2)}) copy-start(f32[256,4096]{1,0:T(8,128)} %get-tuple-element.88) | copy-start | bytes 12582916
  299.6 11.3 %copy-start.25 = (bf16[256,1024]{1,0:T(8,128)(2,1)}, bf16[256,1024]{1,0:T(8,128)(2,1)S(1)}, u32[]{:S(2)}) copy-start(bf16[256,1024]{1,0:T(8,128)(2,1)S(1)} %get-tuple-element.82) | copy-start | bytes 1572868
  299.6 11.3 %copy-start.4 = (f32[256,1024]{1,0:T(8,128)S(1)}, f32[256,1024]{1,0:T(8,128)}, u32[]{:S(2)}) copy-start(f32[256,1024]{1,0:T(8,128)} %copy-done.2) | copy-start | bytes 3145732
  299.6 11.3 %copy-start.7 = (f32[256,1024]{1,0:T(8,128)S(1)}, f32[256,1024]{1,0:T(8,128)}, u32[]{:S(2)}) copy-start(f32[256,1024]{1,0:T(8,128)} %copy-done.6) | copy-start | bytes 3145732
  310.9 6.3 %copy-start.28 = (bf16[256,4096]{1,0:T(8,128)(2,1)}, bf16[256,4096]{1,0:T(8,128)(2,1)S(1)}, u32[]{:S(2)}) copy-start(bf16[256,4096]{1,0:T(8,128)(2,1)S(1)} %get-tuple-element.78) | copy-start | bytes 6291460
  317.2 1.0 copy-start.30
  318.2 6.0 copy-start.27
  327.0 2.5 copy-start.15
  328.8 1.1 copy-start.17
  328.8 1.9 copy-start.11
  328.8 1.9 copy-start.21
  331.5 2.4 copy-start.19
  333.7 3.0 copy-start.20
  333.7 4.9 copy-start.5
  336.7 18.4 %collective-permute-start.2 = (bf16[1024,1536]{1,0:T(8,128)(2,1)}, bf16[1024,1536]{1,0:T(8,128)(2,1)}, u32[]{:S(2)}, u32[]{:S(2)}) collective-permute-start(bf16[1024,1536]{1,0:T(8,128)(2,1)} %convolution_convert_fusion.1), channel_id=1, source_target_pairs={{0,16},{16,0},{1,17},{17,1},{2,18},{18,2},{3,19},{19,3},{4,20},{20... | collective-permute-start | bytes 9437192 | tf_op jit(solution)/shard_map/ppermute | solution.py:36
  343.2 40.8 %collective-permute-start.4 = (bf16[1024,2048]{1,0:T(8,128)(2,1)}, bf16[1024,2048]{1,0:T(8,128)(2,1)}, u32[]{:S(2)}, u32[]{:S(2)}) collective-permute-start(bf16[1024,2048]{1,0:T(8,128)(2,1)} %convolution_convert_fusion.2), channel_id=1, source_target_pairs={{0,16},{16,0},{1,17},{17,1},{2,18},{18,2},{3,19},{19,3},{4,20},{20... | collective-permute-start | bytes 12582920 | tf_op jit(solution)/shard_map/ppermute | solution.py:36
  346.2 6.0 collective-permute-start.3
  351.7 64.2 %collective-permute-start.5 = (bf16[4096,512]{1,0:T(8,128)(2,1)}, bf16[4096,512]{1,0:T(8,128)(2,1)}, u32[]{:S(2)}, u32[]{:S(2)}) collective-permute-start(bf16[4096,512]{1,0:T(8,128)(2,1)} %convolution_convert_fusion), channel_id=1, source_target_pairs={{0,16},{16,0},{1,17},{17,1},{2,18},{18,2},{3,19},{19,3},{4,20},{20... | collective-permute-start | bytes 12582920 | tf_op jit(solution)/shard_map/ppermute | solution.py:36
  380.1 3.8 copy-start.29
  412.0 3.9 copy-start.9
  412.0 3.9 copy-start.26
  415.9 5.7 copy-start.24
  576.5 20.4 %collective-permute-start.6 = (bf16[784,512]{1,0:T(8,128)(2,1)}, bf16[784,512]{1,0:T(8,128)(2,1)S(1)}, u32[]{:S(2)}, u32[]{:S(2)}) collective-permute-start(bf16[784,512]{1,0:T(8,128)(2,1)} %reduce-scatter.2.cloned.1.call-done), channel_id=1, source_target_pairs={{0,32},{32,0},{1,33},{33,1},{2,34},{34,2},{3,35},{35,3},{4,36},{36... | collective-permute-start | bytes 2408456 | tf_op jit(solution)/shard_map/ppermute | solution.py:40
  598.2 8.3 %collective-permute-start.7 = (f32[784,512]{1,0:T(8,128)S(1)}, f32[784,512]{1,0:T(8,128)}, u32[]{:S(2)}, u32[]{:S(2)}) collective-permute-start(f32[784,512]{1,0:T(8,128)S(1)} %convert_add_fusion), channel_id=1, source_target_pairs={{0,16},{16,0},{1,17},{17,1},{2,18},{18,2},{3,19},{19,3},{4,20},{20... | collective-permute-start | bytes 4816904 | tf_op jit(solution)/shard_map/ppermute | solution.py:36
  610.2 2.7 copy-start.1
  611.6 1.0 copy-start.32
  611.6 1.3 copy-start.33
Sparse Core Ops, SparseCore 0:
  16.6 96.4 all-gather.1
  482.7 93.7 reduce-scatter.1

commit v2 on v1

v2 whole, which is shorter than its diff:
```python
import jax
import jax.numpy as jnp
from jax import lax
from jax.experimental import pallas as pl
from jax.experimental.pallas import tpu as pltpu
from jax.sharding import Mesh
from jax.sharding import PartitionSpec as P

HEADS = 16
HEAD_DIM = 64
LEN = 128
ROWS = 256
WIDTH = 1024
HIDDEN = 4096
BLOCK = 512
SCALE = HEAD_DIM ** (-0.5)
EPSILON = 1e-06
ROOT_HALF = 0.5**0.5
NORMAL_PEAK = 0.3989422804014327
LIMIT = 48 * 1024 * 1024

VECTORS_AT = 12288
GATHERED = 12416
O_AT, U_AT, Z_AT, HALF_ALL = 1536, 2048, 4096, 4608
DOWN_AT, EXTRA_AT, GRAD_ALL = 4096, 6144, 6272

F32 = jnp.float32
BF16 = jnp.bfloat16


def dot(left, right):
    return jnp.dot(left, right, preferred_element_type=F32)


def dot_back(left, right):
    return lax.dot_general(left, right, (((1,), (1,)), ((), ())), preferred_element_type=F32)


def dot_rows(left, right):
    return lax.dot_general(left, right, (((0,), (0,)), ((), ())), preferred_element_type=F32)


def swap_cores(value):
    return lax.ppermute(value, "core", [(0, 1), (1, 0)])


def swap_far(value):
    return lax.ppermute(value, "far", [(0, 1), (1, 0)])


def mean(values):
    return jnp.mean(values, -1, keepdims=True)


def normalise(totals):
    centred = totals - mean(totals)
    inverse = lax.rsqrt(mean(centred * centred) + EPSILON)
    return centred * inverse, inverse


def norm_backward(upstream, normed, inverse, gain_row):
    scaled = upstream * gain_row
    return inverse * (scaled - mean(scaled) - normed * mean(scaled * normed))


def soft_of(queries, keys):
    scores = dot_back(queries, keys) * SCALE
    weights = jnp.exp(scores - jnp.max(scores, -1, keepdims=True))
    return weights / jnp.sum(weights, -1, keepdims=True)


def down_rows(block):
    return jnp.concatenate(
        [
            block[32 * part : 32 * part + 32, WIDTH * group : WIDTH * (group + 1)]
            for part in range(4)
            for group in range(4)
        ],
        0,
    )


def forward_kernel(
    x_ref, column_ref, row_ref, bias_ref, pairs_ref,
    y_ref, p_ref, c_ref, hidden_ref, e_ref, slope_ref, n_one_ref, r_one_ref, n_two_ref, r_two_ref,
    total_ref,
):
    step = pl.program_id(0)

    @pl.when(step < 6)
    def _():
        at = pl.multiple_of(step * BLOCK, BLOCK)
        p_ref[:, pl.ds(at, BLOCK)] = (dot(x_ref[...], column_ref[...]) + bias_ref[...]).astype(BF16)

    @pl.when(step == 5)
    def _():
        for seq in range(ROWS // LEN):
            rows = slice(seq * LEN, (seq + 1) * LEN)
            for pair in range(HEADS // 2):
                both = []
                for head in (2 * pair, 2 * pair + 1):
                    q, k, v = (
                        p_ref[rows, part * WIDTH + head * HEAD_DIM : part * WIDTH + (head + 1) * HEAD_DIM]
                        for part in range(3)
                    )
                    both.append(dot(soft_of(q, k).astype(BF16), v))
                c_ref[rows, pair * 128 : (pair + 1) * 128] = jnp.concatenate(both, 1).astype(BF16)

    @pl.when((step >= 6) & (step < 8))
    def _():
        at = pl.multiple_of((step - 6) * BLOCK, BLOCK)
        total_ref[:, pl.ds(at, BLOCK)] = x_ref[:, pl.ds(at, BLOCK)].astype(F32) + (
            dot(c_ref[...], column_ref[...]) + bias_ref[...]
        )

    @pl.when(step == 7)
    def _():
        normed, inverse = normalise(total_ref[...])
        n_one_ref[...] = normed
        r_one_ref[...] = jnp.broadcast_to(inverse, (ROWS, 128))
        hidden = normed * pairs_ref[4:5] + pairs_ref[5:6]
        hidden_ref[...] = hidden.astype(BF16)
        total_ref[...] = hidden + pairs_ref[3:4]

    @pl.when(step >= 8)
    def _():
        upper = dot(hidden_ref[...], column_ref[...]) + bias_ref[...]
        share = 0.5 * (1.0 + lax.erf(upper * ROOT_HALF))
        active = (upper * share).astype(BF16)
        e_ref[...] = active
        slope_ref[...] = (
            share + upper * (NORMAL_PEAK * jnp.exp(-0.5 * upper * upper))
        ).astype(BF16)
        total_ref[...] += dot(active, down_rows(row_ref[...]))

    @pl.when(step == 15)
    def _():
        normed, inverse = normalise(total_ref[...])
        n_two_ref[...] = normed
        r_two_ref[...] = jnp.broadcast_to(inverse, (ROWS, 128))
        y_ref[...] = (normed * pairs_ref[6:7] + pairs_ref[7:8]).astype(BF16)


def whole(shape):
    return pl.BlockSpec(shape, lambda step: (0,) * len(shape))


def shaped(*dims, kind=BF16):
    return jax.ShapeDtypeStruct(dims, kind)


def layer_forward(rows16, gathered, biases, pairs):
    later = lambda step: (0, jnp.maximum(step - 8, 0))
    return pl.pallas_call(
        forward_kernel,
        grid=(16,),
        in_specs=[
            whole((ROWS, WIDTH)),
            pl.BlockSpec((WIDTH, BLOCK), lambda step: (0, step)),
            pl.BlockSpec((128, HIDDEN), lambda step: (jnp.maximum(step - 8, 0), 2)),
            pl.BlockSpec((1, BLOCK), lambda step: (0, step)),
            whole((8, WIDTH)),
        ],
        out_specs=[
            whole((ROWS, WIDTH)),
            whole((ROWS, 3 * WIDTH)),
            whole((ROWS, WIDTH)),
            whole((ROWS, WIDTH)),
            pl.BlockSpec((ROWS, BLOCK), later),
            pl.BlockSpec((ROWS, BLOCK), later),
            whole((ROWS, WIDTH)),
            whole((ROWS, 128)),
            whole((ROWS, WIDTH)),
            whole((ROWS, 128)),
        ],
        out_shape=[
            shaped(ROWS, WIDTH),
            shaped(ROWS, 3 * WIDTH),
            shaped(ROWS, WIDTH),
            shaped(ROWS, WIDTH),
            shaped(ROWS, HIDDEN),
            shaped(ROWS, HIDDEN),
            shaped(ROWS, WIDTH, kind=F32),
            shaped(ROWS, 128, kind=F32),
            shaped(ROWS, WIDTH, kind=F32),
            shaped(ROWS, 128, kind=F32),
        ],
        scratch_shapes=[pltpu.VMEM((ROWS, WIDTH), F32)],
        compiler_params=pltpu.CompilerParams(vmem_limit_bytes=LIMIT),
        cost_estimate=pl.CostEstimate(
            flops=2 * ROWS * 12 * WIDTH * WIDTH, bytes_accessed=32 << 20, transcendentals=0
        ),
        name="layer_forward",
    )(rows16, gathered, gathered, biases, pairs)


def backward_kernel(
    upstream_ref, column_ref, row_ref, pairs_ref, p_ref, slope_ref,
    n_one_ref, r_one_ref, n_two_ref, r_two_ref,
    x_grad_ref, halves_ref, pair_grads_ref, up_grads_ref,
    z_ref, o_ref, p_grad_ref, branch_ref, total_ref,
):
    step = pl.program_id(0)

    def column_sums(values):
        return jnp.sum(values, 0, keepdims=True)

    @pl.when(step == 0)
    def _():
        upstream = upstream_ref[...].astype(F32)
        normed = n_two_ref[...]
        pair_grads_ref[6:7] = column_sums(upstream * normed)
        pair_grads_ref[7:8] = column_sums(upstream)
        grad = norm_backward(upstream, normed, r_two_ref[:, 0:1], pairs_ref[6:7])
        total_ref[...] = grad
        rounded = grad.astype(BF16)
        z_ref[...] = rounded
        pair_grads_ref[3:4] = column_sums(rounded.astype(F32))
        halves_ref[0, :, Z_AT:] = rounded[:, :512]
        halves_ref[1, :, Z_AT:] = rounded[:, 512:]

    @pl.when(step < 8)
    def _():
        active_grad = dot_back(z_ref[...], down_rows(row_ref[...]))
        upper_grad = (active_grad * slope_ref[...].astype(F32)).astype(BF16)
        up_grads_ref[...] = column_sums(upper_grad.astype(F32))
        at = pl.multiple_of(U_AT + lax.rem(step, 4) * BLOCK, BLOCK)
        halves_ref[step // 4, :, pl.ds(at, BLOCK)] = upper_grad
        total_ref[...] += dot_back(upper_grad, column_ref[...])

    @pl.when(step == 7)
    def _():
        hidden_grad = total_ref[...]
        normed = n_one_ref[...]
        pair_grads_ref[4:5] = column_sums(hidden_grad * normed)
        pair_grads_ref[5:6] = column_sums(hidden_grad)
        grad = norm_backward(hidden_grad, normed, r_one_ref[:, 0:1], pairs_ref[4:5])
        branch_ref[...] = grad
        rounded = grad.astype(BF16)
        o_ref[...] = rounded
        pair_grads_ref[2:3] = column_sums(rounded.astype(F32))
        halves_ref[0, :, O_AT:U_AT] = rounded[:, :512]
        halves_ref[1, :, O_AT:U_AT] = rounded[:, 512:]

    @pl.when(step == 8)
    def _():
        total_ref[...] = dot_back(o_ref[:, :BLOCK], column_ref[...])

    @pl.when(step == 9)
    def _():
        attended_grad = (total_ref[...] + dot_back(o_ref[:, BLOCK:], column_ref[...])).astype(BF16)
        z_ref[...] = attended_grad
        for seq in range(ROWS // LEN):
            rows = slice(seq * LEN, (seq + 1) * LEN)
            for pair in range(HEADS // 2):
                both = []
                for head in (2 * pair, 2 * pair + 1):
                    lanes = slice(head * HEAD_DIM, (head + 1) * HEAD_DIM)
                    q, k, v = (
                        p_ref[rows, part * WIDTH + head * HEAD_DIM : part * WIDTH + (head + 1) * HEAD_DIM]
                        for part in range(3)
                    )
                    grad = z_ref[rows, lanes]
                    soft = soft_of(q, k)
                    value_grad = dot_rows(soft.astype(BF16), grad)
                    soft_grad = dot_back(grad, v)
                    weighed = soft_grad * soft
                    scores_grad = (
                        weighed - soft * jnp.sum(weighed, -1, keepdims=True)
                    ).astype(BF16)
                    both.append(
                        (
                            dot(scores_grad, k) * SCALE,
                            dot_rows(scores_grad, q) * SCALE,
                            value_grad,
                        )
                    )
                for part in range(3):
                    p_grad_ref[
                        rows, part * WIDTH + pair * 128 : part * WIDTH + (pair + 1) * 128
                    ] = jnp.concatenate([both[0][part], both[1][part]], 1).astype(BF16)
        halves_ref[0, :, :O_AT] = p_grad_ref[:, :O_AT]
        halves_ref[1, :, :O_AT] = p_grad_ref[:, O_AT:]
        pair_grads_ref[0:1] = column_sums(p_grad_ref[:, :WIDTH].astype(F32))
        pair_grads_ref[1:2] = column_sums(p_grad_ref[:, 2 * WIDTH :].astype(F32))
        total_ref[...] = branch_ref[...]

    @pl.when(step >= 10)
    def _():
        at = pl.multiple_of((step - 10) * BLOCK, BLOCK)
        total_ref[...] += dot_back(p_grad_ref[:, pl.ds(at, BLOCK)], column_ref[...])

    @pl.when(step == 15)
    def _():
        x_grad_ref[...] = total_ref[...].astype(BF16)


def layer_backward(upstream, gathered, pairs, kept):
    p, slope, n_one, r_one, n_two, r_two = kept
    early = lambda step: (0, jnp.minimum(step, 7))
    column = lambda step: (0, jnp.where(step < 8, step + 8, jnp.where(step < 10, step - 2, step - 10)))
    return pl.pallas_call(
        backward_kernel,
        grid=(16,),
        in_specs=[
            whole((ROWS, WIDTH)),
            pl.BlockSpec((WIDTH, BLOCK), column),
            pl.BlockSpec((128, HIDDEN), lambda step: (jnp.minimum(step, 7), 2)),
            whole((8, WIDTH)),
            whole((ROWS, 3 * WIDTH)),
            pl.BlockSpec((ROWS, BLOCK), early),
            whole((ROWS, WIDTH)),
            whole((ROWS, 128)),
            whole((ROWS, WIDTH)),
            whole((ROWS, 128)),
        ],
        out_specs=[
            whole((ROWS, WIDTH)),
            whole((2, ROWS, HALF_ALL)),
            whole((8, WIDTH)),
            pl.BlockSpec((1, BLOCK), early),
        ],
        out_shape=[
            shaped(ROWS, WIDTH),
            shaped(2, ROWS, HALF_ALL),
            shaped(8, WIDTH, kind=F32),
            shaped(1, HIDDEN, kind=F32),
        ],
        scratch_shapes=[
            pltpu.VMEM((ROWS, WIDTH), BF16),
            pltpu.VMEM((ROWS, WIDTH), BF16),
            pltpu.VMEM((ROWS, 3 * WIDTH), BF16),
            pltpu.VMEM((ROWS, WIDTH), F32),
            pltpu.VMEM((ROWS, WIDTH), F32),
        ],
        compiler_params=pltpu.CompilerParams(vmem_limit_bytes=LIMIT),
        cost_estimate=pl.CostEstimate(
            flops=2 * ROWS * 12 * WIDTH * WIDTH, bytes_accessed=32 << 20, transcendentals=0
        ),
        name="layer_backward",
    )(upstream, gathered, gathered, pairs, p, slope, n_one, r_one, n_two, r_two)


def weight_grads_kernel(x_ref, c_ref, h_ref, e_ref, lefts_ref, x2_ref, c2_ref, h2_ref, e2_ref, rights_ref, extra_ref, out_ref):
    def product(one_ref, two_ref, at, end):
        return (
            dot_rows(one_ref[...], lefts_ref[:, at:end])
            + dot_rows(two_ref[...], rights_ref[:, at:end])
        ).astype(BF16)

    out_ref[:, :O_AT] = product(x_ref, x2_ref, 0, O_AT)
    out_ref[:, O_AT:U_AT] = product(c_ref, c2_ref, O_AT, U_AT)
    out_ref[:, U_AT:Z_AT] = product(h_ref, h2_ref, U_AT, Z_AT)
    down = product(e_ref, e2_ref, Z_AT, HALF_ALL)
    for part in range(4):
        for group in range(4):
            at = part * 256 + group * 64
            out_ref[
                part * 64 : part * 64 + 64, DOWN_AT + group * 512 : DOWN_AT + (group + 1) * 512
            ] = down[at : at + 64]
    out_ref[:, EXTRA_AT:] = extra_ref[...]


def weight_grads(own, own_half, other, other_half, extra):
    narrow = pl.BlockSpec((ROWS, 256), lambda step: (0, step))
    wide = pl.BlockSpec((ROWS, 1024), lambda step: (0, step))
    tokens = [narrow, narrow, narrow, wide, whole((ROWS, HALF_ALL))]
    return pl.pallas_call(
        weight_grads_kernel,
        grid=(4,),
        in_specs=[*tokens, *tokens, pl.BlockSpec((256, 128), lambda step: (step, 0))],
        out_specs=pl.BlockSpec((256, GRAD_ALL), lambda step: (step, 0)),
        out_shape=shaped(WIDTH, GRAD_ALL),
        compiler_params=pltpu.CompilerParams(vmem_limit_bytes=LIMIT),
        cost_estimate=pl.CostEstimate(
            flops=2 * ROWS * 12 * WIDTH * WIDTH, bytes_accessed=24 << 20, transcendentals=0
        ),
        name="weight_grads",
    )(*own, own_half, *other, other_half, extra)


def finish_kernel(low_ref, high_ref, project_ref, output_ref, up_ref, down_ref):
    for half, ref in enumerate((low_ref, high_ref)):
        project_ref[:, half * 1536 : (half + 1) * 1536] = ref[:, :O_AT]
        output_ref[:, half * 512 : (half + 1) * 512] = ref[:, O_AT:U_AT]
        up_ref[:, half * 2048 : (half + 1) * 2048] = ref[:, U_AT:Z_AT]
        for group in range(4):
            at = DOWN_AT + group * 512
            down_ref[group * 64 : group * 64 + 64, half * 512 : (half + 1) * 512] = ref[
                :, at : at + 512
            ]


def finish(low, high):
    return pl.pallas_call(
        finish_kernel,
        out_shape=[
            shaped(64, 3 * WIDTH, kind=F32),
            shaped(64, WIDTH, kind=F32),
            shaped(64, HIDDEN, kind=F32),
            shaped(256, WIDTH, kind=F32),
        ],
        compiler_params=pltpu.CompilerParams(vmem_limit_bytes=LIMIT),
        name="finish",
    )(low, high)


def gather_weights(project, output, upward, downward, vectors):
    core = lax.axis_index("core")
    half = lax.dynamic_slice_in_dim(
        jnp.concatenate([project, output, upward], 1), core * 32, 32, 0
    )
    down = lax.dynamic_slice_in_dim(downward, core * 128, 128, 0)
    down = down.reshape(4, 32, WIDTH).transpose(1, 0, 2).reshape(32, HIDDEN)
    flat = jnp.concatenate(vectors).reshape(6, 128)
    extra = jnp.concatenate([flat, jnp.zeros((26, 128), BF16)], 0)
    packed = jnp.concatenate([half, down, extra], 1)
    gathered = lax.all_gather(packed, ("z", "y", "core"), axis=0, tiled=True)
    rows = gathered[:, VECTORS_AT:].reshape(16, 64, 128)[:, :6].astype(F32)
    pairs = rows[:, :4].reshape(16, 8, 64).transpose(1, 0, 2).reshape(8, WIDTH)
    ups = rows[:, 4:].reshape(1, HIDDEN)
    biases = jnp.concatenate(
        [pairs[0:1], jnp.zeros((1, WIDTH), F32), pairs[1:2], pairs[2:3], ups], 1
    )
    return gathered, biases, pairs


def reduce_grads(own, halves, other, pair_grads, up_grads):
    core = lax.axis_index("core")
    other_half = swap_cores(lax.dynamic_index_in_dim(halves, 1 - core, 0, keepdims=False))
    own_half = lax.dynamic_index_in_dim(halves, core, 0, keepdims=False)
    rows = jnp.concatenate(
        [
            pair_grads.reshape(8, 16, 64).transpose(1, 0, 2).reshape(16, 4, 128),
            up_grads.reshape(16, 2, 128),
        ],
        1,
    ).astype(BF16)
    extra = jnp.concatenate([rows, jnp.zeros((16, 58, 128), BF16)], 1).reshape(WIDTH, 128)
    packed = weight_grads(own, own_half, other, other_half, extra)
    owned = lax.psum_scatter(packed, ("z", "y"), scatter_dimension=0, tiled=True)
    owned = lax.optimization_barrier(owned)
    total = owned.astype(F32) + swap_far(owned).astype(F32)
    total = lax.optimization_barrier(total)
    sibling = swap_cores(total)
    low = jnp.where(core == 0, total, sibling)
    high = jnp.where(core == 0, sibling, total)
    project, output, upward, downward = finish(low, high)
    vectors = (total[:6, EXTRA_AT:] + sibling[:6, EXTRA_AT:]).reshape(768)
    narrow = [vectors[64 * k : 64 * (k + 1)][None] for k in range(8)]
    query, value, output_b, down_b, gain_one, shift_one, gain_two, shift_two = narrow
    return (
        project[None],
        output[None],
        upward[None],
        downward[None],
        query,
        value,
        output_b,
        vectors[512:768][None],
        down_b,
        gain_one,
        shift_one,
        gain_two,
        shift_two,
    )


def on_device(
    layer_input,
    cotangent,
    project_weight,
    output_weight,
    up_weight,
    down_weight,
    query_bias,
    value_bias,
    output_bias,
    up_bias,
    down_bias,
    first_gain,
    first_shift,
    second_gain,
    second_shift,
):
    first_section = lax.axis_index("section") == 0
    gathered, biases, pairs = gather_weights(
        project_weight[0],
        output_weight[0],
        up_weight[0],
        down_weight[0],
        (
            query_bias[0],
            value_bias[0],
            output_bias[0],
            down_bias[0],
            first_gain[0],
            first_shift[0],
            second_gain[0],
            second_shift[0],
            up_bias[0],
        ),
    )
    shape = layer_input.shape
    own_rows = layer_input.reshape(-1, WIDTH)
    own_grad = cotangent.reshape(-1, WIDTH)

    early = layer_forward(own_rows, gathered, biases, pairs)[0]
    received = lax.ppermute(early, "section", [(0, 1)])
    rows16 = jnp.where(first_section, own_rows, received)
    result, p, c, hidden, e, slope, n_one, r_one, n_two, r_two = layer_forward(
        rows16, gathered, biases, pairs
    )
    kept = (p, slope, n_one, r_one, n_two, r_two)
    own = (rows16, c, hidden, e)
    other = tuple(swap_cores(array) for array in own)

    early_grad = layer_backward(own_grad, gathered, pairs, kept)[0]
    back = lax.ppermute(early_grad, "section", [(1, 0)])
    upstream = jnp.where(first_section, back, own_grad)
    rows_grad, halves, pair_grads, up_grads = layer_backward(upstream, gathered, pairs, kept)
    return (
        result.reshape(1, *shape),
        rows_grad.reshape(1, *shape),
        *reduce_grads(own, halves, other, pair_grads, up_grads),
    )


def solution(mesh):
    devices = mesh.devices.reshape(2, 2, 2, 4, 4)
    fine = Mesh(devices, ("section", "far", "core", "z", "y"))
    shard = ("z", "y")
    seqs = P(None, ("far", "core", "z", "y"), None, None)
    matrix = P("section", shard, None)
    vector = P("section", shard)
    rows = P("section", None, ("far", "core", "z", "y"), None, None)
    return jax.shard_map(
        on_device,
        mesh=fine,
        in_specs=(seqs, seqs, *([matrix] * 4), *([vector] * 9)),
        out_specs=(rows, rows, *([matrix] * 4), *([vector] * 9)),
        check_vma=False,
    )
```

time: 630 us -> 447 us (0.71)
  local copies, waits for them, and re-layouts: 187 us -> 9.75 us
  matrix products: 152 us -> 0 us
  Pallas kernels: 0 us -> 152 us
  other arithmetic: 21.6 us -> 7.84 us
  waiting for transfers between devices: 233 us -> 243 us
    pallas_call x0 -> x6, Pallas kernels: none -> 152 us  [the longest x2 72.4 us: layer_backward(): pl.pallas_call(backward_kernel, grid=(16,), in_specs=[whole((ROWS, WIDTH)...]
    dot_general x34 -> x0, matrix products: 152 us -> none  [the longest x7 53.3 us: matmul(): return jnp.dot(left, right, preferred_element_type=F32)]
    concatenate x3 -> x1, local copies, waits for them, and re-layouts: 61 us -> 0.01 us  [gather_weights(): jnp.concatenate([pairs[0:1], jnp.zeros((1, WIDTH), F32), pairs[1:2], pair...]
    reshape x11 -> x2, local copies, waits for them, and re-layouts: 48.9 us -> 0.19 us  [reduce_grads(): pair_grads.reshape(8, 16, 64).transpose(1, 0, 2).reshape(16, 4, 128)]
    slice x9 -> x6, local copies, waits for them, and re-layouts: 37.1 us -> 1.28 us  [the longest x1 0.97 us: gather_weights(): rows = gathered[:, VECTORS_AT:].reshape(16, 64, 128)[:, :6].astype(F32)]
    unnamed x102 -> x38, local copies, waits for them, and re-layouts: 17.2 us -> 1.8 us
    ppermute x5 -> x6, waiting for transfers between devices: 0.27 us -> 11.2 us  [swap_cores(): return lax.ppermute(value, 'core', [(0, 1), (1, 0)])]
    transpose x2, local copies, waits for them, and re-layouts: 10.3 us -> 0.03 us  [the longest x1 0.01 us: gather_weights(): pairs = rows[:, :4].reshape(16, 8, 64).transpose(1, 0, 2).reshape(8, WIDTH)]
  transfers between devices with their start and end apart: 10 -> 11, of which waited for: 6 -> 9; matrix products, arithmetic and copies ran while one was open for 13% -> 0% of each run, Pallas kernels for 0% -> 0%
where the time goes in v2:
time: 447 us; the launch traced here: 440 us
  waiting for transfers between devices  243 us (54%)
  Pallas kernels  152 us (34%)
  between operations  14.6 us (3%)
  starting transfers between devices  12.8 us (3%)
  local copies, waits for them, and re-layouts  9.75 us (2%)
  other arithmetic  7.84 us (2%)
    all_gather x1, waiting for transfers between devices, gather_weights(): gathered = lax.all_gather(packed, ('z', 'y', 'core'), axis=0, tiled=True)  96.6 us
    reduce_scatter x1, waiting for transfers between devices, reduce_grads(): lax.psum_scatter(packed, ('z', 'y'), scatter_dimension=0, tiled=True)  94 us
    pallas_call x2, Pallas kernels, layer_backward(): pl.pallas_call(backward_kernel, grid=(16,), in_specs=[whole((ROWS, WIDTH)...  72.4 us
    pallas_call x2, Pallas kernels, layer_forward(): pl.pallas_call(forward_kernel, grid=(16,), in_specs=[whole((ROWS, WIDTH))...  64.9 us
    ppermute x1, waiting for transfers between devices, swap_far(): return lax.ppermute(value, 'far', [(0, 1), (1, 0)])  17.4 us
    ppermute x1, waiting for transfers between devices, on_device(): back = lax.ppermute(early_grad, 'section', [(1, 0)])  13.5 us
    pallas_call x1, Pallas kernels, weight_grads(): pl.pallas_call(weight_grads_kernel, grid=(4,), in_specs=[*tokens, *tokens...  12.5 us
    ppermute x6, waiting for transfers between devices, swap_cores(): return lax.ppermute(value, 'core', [(0, 1), (1, 0)])  11.2 us
  transfers between devices with their start and end apart: 11, of which 9 were waited for; matrix products, arithmetic and copies ran while one was open for 0% of the time, Pallas kernels for 0%

profile of v2, /device:TPU:1, one launch (start us, length us, event | category | flops | bytes accessed | tf_op | source)
XLA Modules:
  0.0 440.0 jit_solution(146259221966082935)
XLA Ops:
  7.2 0.0 copy-start
  7.2 0.0 copy-start.13
  7.2 0.0 copy-start.14
  7.2 0.0 copy-start.15
  7.2 0.0 copy-start.16
  7.2 0.0 copy-start.9
  7.3 0.0 all-gather.2.cloned.1.call-start
  7.3 0.9 copy-done
  8.3 0.7 reduce
  9.0 1.1 fusion.3
  10.2 0.1 concatenate.23
  10.3 0.9 fusion.1
  11.2 0.0 all-gather.2.cloned.1.call-update
  11.2 0.0 reduce-scatter.2.cloned.1.call-start
  11.3 96.6 %all-gather.2.cloned.1.call-done.column_ref.row_ref = bf16[1024,12416]{1,0:T(8,128)(2,1)} async-done(((bf16[32,12416]{1,0:T(8,128)(2,1)}), bf16[1024,12416]{1,0:T(8,128)(2,1)}) %all-gather.2.cloned.1.call-update) | async-done | bytes 25427984 | tf_op jit(solution)/shard_map/all_gather | solution.py:418
  107.9 1.0 slice.85
  108.9 0.1 reshape.93
  109.0 0.1 slice_reduce_fusion
  109.1 0.1 slice.68
  109.2 0.1 slice.70
  109.3 0.1 slice.72
  109.4 0.1 reshape.95.pairs_ref
  109.5 33.1 %layer_forward.2 = (bf16[256,1024]{1,0:T(8,128)(2,1)S(1)}, bf16[256,3072]{1,0:T(8,128)(2,1)}, bf16[256,1024]{1,0:T(8,128)(2,1)}, bf16[256,1024]{1,0:T(8,128)(2,1...) custom-call(bf16[256,1024]{1,0:T(8,128)(2,1)S(1)} %bitcast.59, ...), custom_call_target="tpu_custom_call" | custom-call | flops 6442450944 | bytes 33554432 | tf_op jit(solution)/shard_map/layer_forward/pallas_call | solution.py:154
  142.6 3.6 collective-permute-start
  146.2 10.5 %collective-permute-done = bf16[256,1024]{1,0:T(8,128)(2,1)S(1)} collective-permute-done((bf16[256,1024]{1,0:T(8,128)(2,1)S(1)}, bf16[256,1024]{1,0:T(8,128)(2,1)S(1)}, u32[]{:S(2)}, u32[]{:S(2)}) %collective-permute-start) | collective-permute-done | bytes 524320 | tf_op jit(solution)/shard_map/ppermute | solution.py:509
  156.7 0.1 broadcast_select_fusion.3.x_ref
  156.8 0.0 copy-start.5
  156.8 31.8 %layer_forward.3 = (bf16[256,1024]{1,0:T(8,128)(2,1)}, bf16[256,3072]{1,0:T(8,128)(2,1)S(1)}, bf16[256,1024]{1,0:T(8,128)(2,1)S(1)}, bf16[256,1024]{1,0:T(8,128)...) custom-call(bf16[256,1024]{1,0:T(8,128)(2,1)S(1)} %broadcast_select_, ...), custom_call_target="tpu_custom_call" | custom-call | flops 6442450944 | bytes 33554432 | tf_op jit(solution)/shard_map/layer_forward/pallas_call | solution.py:154
  188.7 0.8 copy-done.7
  189.5 36.3 %layer_backward.2 = (bf16[256,1024]{1,0:T(8,128)(2,1)}, bf16[2,256,4608]{2,1,0:T(8,128)(2,1)}, f32[8,1024]{1,0:T(8,128)}, f32[1,4096]{1,0:T(1,128)}) custom-call(bf16[256,1024]{1,0:T(8,128)(2,1)S(1)} %bitcast.60, bf16[1024,12416]{1,0:T(8,128)(2,1)} %all-gather.2.cloned.1.call-done.column_ref.row_ref, ...), custom_call_target="tpu_custom_call" | custom-call | flops 6442450944 | bytes 33554432 | tf_op jit(solution)/shard_map/layer_backward/pallas_call | solution.py:302
  225.7 1.3 collective-permute-start.1
  227.0 0.0 copy-start.3
  227.0 13.5 %collective-permute-done.1 = bf16[256,1024]{1,0:T(8,128)(2,1)} collective-permute-done((bf16[256,1024]{1,0:T(8,128)(2,1)}, bf16[256,1024]{1,0:T(8,128)(2,1)}, u32[]{:S(2)}, u32[]{:S(2)}) %collective-permute-start.1) | collective-permute-done | bytes 524320 | tf_op jit(solution)/shard_map/ppermute | solution.py:519
  240.5 1.3 broadcast_select_fusion.2.upstream_ref
  241.8 36.1 %layer_backward.3 = (bf16[256,1024]{1,0:T(8,128)(2,1)}, bf16[2,256,4608]{2,1,0:T(8,128)(2,1)}, f32[8,1024]{1,0:T(8,128)S(1)}, f32[1,4096]{1,0:T(1,128)S(1)}) custom-call(bf16[256,1024]{1,0:T(8,128)(2,1)S(1)} %broadcast_select_fusion.2.upstream_ref, bf16[1024,12416]{1,0:T(8,128)(2,1)} %all-gather.2.cloned.1.call-done.column_ref.row_ref, ...), custom_call_target="tpu_custom_call" | custom-call | flops 6442450944 | bytes 33554432 | tf_op jit(solution)/shard_map/layer_backward/pallas_call | solution.py:302
  277.9 5.0 %dynamic-slice_bitcast_fusion = (bf16[256,4608]{1,0:T(8,128)(2,1)}, bf16[256,4608]{1,0:T(8,128)(2,1)}) fusion(bf16[2,256,4608]{2,1,0:T(8,128)(2,1)} %get-tuple-element.48, s32[]{:T(128)S(6)} %select_n.44, s32[]{:T(128)S(6)} %select_n.43), kind=kLoop, calls=%fused_computation | loop fusion | bytes 9437192 | tf_op jit(solution)/shard_map/jit(dynamic_index_in_dim)/squeeze | solution.py:430
  282.9 1.9 collective-permute-start.6
  284.8 0.0 collective-permute-start.5
  284.8 0.5 collective-permute-start.3
  285.3 0.1 collective-permute-start.4
  285.4 0.7 collective-permute-start.2
  286.0 0.1 reshape.99
  286.1 0.1 reshape.100
  286.2 0.1 convert_reduce_fusion
  286.3 0.1 fusion.6
  286.4 7.1 %collective-permute-done.3.c2_ref = bf16[256,1024]{1,0:T(8,128)(2,1)} collective-permute-done((bf16[256,1024]{1,0:T(8,128)(2,1)S(1)}, bf16[256,1024]{1,0:T(8,128)(2,1)}, u32[]{:S(2)}, u32[]{:S(2)}) %collective-permute-start.3) | collective-permute-done | bytes 524320 | tf_op jit(solution)/shard_map/ppermute | solution.py:44
  293.4 0.7 collective-permute-done.4.h2_ref
  294.1 0.2 collective-permute-done.2.x2_ref
  294.3 0.0 collective-permute-done.5.e2_ref
  294.3 0.0 collective-permute-done.6.rights_ref
  294.3 12.5 %weight_grads.1 = bf16[1024,6272]{1,0:T(8,128)(2,1)} custom-call(bf16[256,1024]{1,0:T(8,128)(2,1)S(1)} %broadcast_select_fusion.3.x_ref, bf16[256,1024]{1,0:T(8,128)(2,1)S(1)} %copy-done.8, bf16[256,1024]{1,0:T(8,128)(2,1)} %get-tuple-element.46.h_ref, bf16[256,4096]{1,0:T(8,128)(2,1)S(1)} %copy-done.6, bf16[256,4608]{1,0:T(8,128)(2,1)} %get-tuple-element.89.lefts_ref, ...), custom_call_target="tpu_custom_call" | custom-call | flops 6442450944 | bytes 25165824 | tf_op jit(solution)/shard_map/weight_grads/pallas_call | solution.py:368
  306.8 0.0 reduce-scatter.2.cloned.1.call-update
  306.9 94.0 %reduce-scatter.2.cloned.1.call-done = bf16[64,6272]{1,0:T(8,128)(2,1)} async-done(((bf16[1024,6272]{1,0:T(8,128)(2,1)}), bf16[64,6272]{1,0:T(8,128)(2,1)}) %reduce-scatter.2.cloned.1.call-update) | async-done | bytes 802832 | tf_op jit(solution)/shard_map/reduce_scatter | solution.py:441
  400.9 2.8 collective-permute-start.7
  403.7 17.4 %collective-permute-done.7 = bf16[64,6272]{1,0:T(8,128)(2,1)S(1)} collective-permute-done((bf16[64,6272]{1,0:T(8,128)(2,1)}, bf16[64,6272]{1,0:T(8,128)(2,1)S(1)}, u32[]{:S(2)}, u32[]{:S(2)}) %collective-permute-start.7) | collective-permute-done | bytes 802848 | tf_op jit(solution)/shard_map/ppermute | solution.py:48
  421.1 1.3 convert_add_fusion
  422.4 1.9 collective-permute-start.8
  424.3 3.2 collective-permute-done.8
  427.5 0.7 slice_add_fusion
  428.2 0.6 slice.79
  428.8 0.6 slice_bitcast_fusion
  429.4 1.6 broadcast_select_fusion
  431.0 0.0 copy-start.1
  431.0 1.9 finish.1
  (36 shorter events, 0.2 us)
Async XLA Ops:
  7.2 1.1 copy-start
  7.2 2.9 copy-start.13
  7.2 2.9 copy-start.14
  7.2 2.9 copy-start.15
  7.2 2.9 copy-start.16
  7.2 2.9 copy-start.9
  7.3 2.9 copy-start.10
  7.3 2.9 copy-start.11
  7.3 2.9 copy-start.12
  7.3 100.6 %all-gather.2.cloned.1.call-start = ((), (), s32[]{:S(2)}) async-start(), calls=%async_computation.1 | async-start | bytes 26222592 | tf_op jit(solution)/shard_map/all_gather | solution.py:418
  10.3 99.2 %copy-start.4 = (bf16[2,1,128,1024]{3,2,1,0:T(8,128)(2,1)S(1)}, bf16[2,1,128,1024]{3,2,1,0:T(8,128)(2,1)}, u32[]{:S(2)}) copy-start(bf16[2,1,128,1024]{3,2,1,0:T(8,128)(2,1)} %param.15) | copy-start | bytes 1572868
  11.2 389.7 %reduce-scatter.2.cloned.1.call-start = ((), (), s32[]{:S(2)}) async-start(), calls=%async_computation.2 | async-start | bytes 13647872 | tf_op jit(solution)/shard_map/reduce_scatter | solution.py:441
  142.6 14.2 %collective-permute-start = (bf16[256,1024]{1,0:T(8,128)(2,1)S(1)}, bf16[256,1024]{1,0:T(8,128)(2,1)S(1)}, u32[]{:S(2)}, u32[]{:S(2)}) collective-permute-start(bf16[256,1024]{1,0:T(8,128)(2,1)S(1)} %get-tuple-element.35), channel_id=1, source_target_pairs={{0,64},{1,65},{2,66},{3,67},{4,68},{5,69},{6,70},{7,71},{8,72},{9,... | collective-permute-start | bytes 1572872 | tf_op jit(solution)/shard_map/ppermute | solution.py:509
  156.8 32.6 %copy-start.5 = (bf16[2,1,128,1024]{3,2,1,0:T(8,128)(2,1)S(1)}, bf16[2,1,128,1024]{3,2,1,0:T(8,128)(2,1)}, u32[]{:S(2)}) copy-start(bf16[2,1,128,1024]{3,2,1,0:T(8,128)(2,1)} %param.16) | copy-start | bytes 1572868
  188.7 0.8 copy-start.7
  189.5 36.3 %copy-start.2 = (f32[256,1024]{1,0:T(8,128)}, f32[256,1024]{1,0:T(8,128)S(1)}, u32[]{:S(2)}) copy-start(f32[256,1024]{1,0:T(8,128)S(1)} %get-tuple-element.41.n_two_ref) | copy-start | bytes 3145732
  225.7 14.8 %collective-permute-start.1 = (bf16[256,1024]{1,0:T(8,128)(2,1)}, bf16[256,1024]{1,0:T(8,128)(2,1)}, u32[]{:S(2)}, u32[]{:S(2)}) collective-permute-start(bf16[256,1024]{1,0:T(8,128)(2,1)} %get-tuple-element.43), channel_id=1, source_target_pairs={{64,0},{65,1},{66,2},{67,3},{68,4},{69,5},{70,6},{71,7},{72,8},{73... | collective-permute-start | bytes 1572872 | tf_op jit(solution)/shard_map/ppermute | solution.py:519
  227.0 14.8 %copy-start.3 = (f32[256,1024]{1,0:T(8,128)S(1)}, f32[256,1024]{1,0:T(8,128)}, u32[]{:S(2)}) copy-start(f32[256,1024]{1,0:T(8,128)} %copy-done.2) | copy-start | bytes 3145732
  277.9 6.8 %copy-start.6 = (bf16[256,4096]{1,0:T(8,128)(2,1)S(1)}, bf16[256,4096]{1,0:T(8,128)(2,1)}, u32[]{:S(2)}) copy-start(bf16[256,4096]{1,0:T(8,128)(2,1)} %get-tuple-element.47.e_ref) | copy-start | bytes 6291460
  277.9 6.8 %copy-start.8 = (bf16[256,1024]{1,0:T(8,128)(2,1)S(1)}, bf16[256,1024]{1,0:T(8,128)(2,1)}, u32[]{:S(2)}) copy-start(bf16[256,1024]{1,0:T(8,128)(2,1)} %copy-done.7) | copy-start | bytes 1572868
  282.9 11.4 %collective-permute-start.6 = (bf16[256,4608]{1,0:T(8,128)(2,1)}, bf16[256,4608]{1,0:T(8,128)(2,1)}, u32[]{:S(2)}, u32[]{:S(2)}) collective-permute-start(bf16[256,4608]{1,0:T(8,128)(2,1)} %get-tuple-element.88), channel_id=1, source_target_pairs={{0,16},{16,0},{1,17},{17,1},{2,18},{18,2},{3,19},{19,3},{4,20},{20... | collective-permute-start | bytes 7077896 | tf_op jit(solution)/shard_map/ppermute | solution.py:44
  284.8 9.5 %collective-permute-start.5 = (bf16[256,4096]{1,0:T(8,128)(2,1)S(1)}, bf16[256,4096]{1,0:T(8,128)(2,1)}, u32[]{:S(2)}, u32[]{:S(2)}) collective-permute-start(bf16[256,4096]{1,0:T(8,128)(2,1)S(1)} %copy-done.6), channel_id=1, source_target_pairs={{0,16},{16,0},{1,17},{17,1},{2,18},{18,2},{3,19},{19,3},{4,20},{20... | collective-permute-start | bytes 6291464 | tf_op jit(solution)/shard_map/ppermute | solution.py:44
  284.8 8.6 %collective-permute-start.3 = (bf16[256,1024]{1,0:T(8,128)(2,1)S(1)}, bf16[256,1024]{1,0:T(8,128)(2,1)}, u32[]{:S(2)}, u32[]{:S(2)}) collective-permute-start(bf16[256,1024]{1,0:T(8,128)(2,1)S(1)} %copy-done.8), channel_id=1, source_target_pairs={{0,16},{16,0},{1,17},{17,1},{2,18},{18,2},{3,19},{19,3},{4,20},{20... | collective-permute-start | bytes 1572872 | tf_op jit(solution)/shard_map/ppermute | solution.py:44
  285.3 8.8 %collective-permute-start.4 = (bf16[256,1024]{1,0:T(8,128)(2,1)}, bf16[256,1024]{1,0:T(8,128)(2,1)}, u32[]{:S(2)}, u32[]{:S(2)}) collective-permute-start(bf16[256,1024]{1,0:T(8,128)(2,1)} %get-tuple-element.46.h_ref), channel_id=1, source_target_pairs={{0,16},{16,0},{1,17},{17,1},{2,18},{18,2},{3,19},{19,3},{4,20},{20... | collective-permute-start | bytes 1572872 | tf_op jit(solution)/shard_map/ppermute | solution.py:44
  285.4 8.9 %collective-permute-start.2 = (bf16[256,1024]{1,0:T(8,128)(2,1)S(1)}, bf16[256,1024]{1,0:T(8,128)(2,1)}, u32[]{:S(2)}, u32[]{:S(2)}) collective-permute-start(bf16[256,1024]{1,0:T(8,128)(2,1)S(1)} %broadcast_select_fusion.3.x_ref), channel_id=1, source_target_pairs={{0,16},{16,0},{1,17},{17,1},{2,18},{18,2},{3,19},{19,3},{4,20},{20... | collective-permute-start | bytes 1572872 | tf_op jit(solution)/shard_map/ppermute | solution.py:44
  400.9 20.2 %collective-permute-start.7 = (bf16[64,6272]{1,0:T(8,128)(2,1)}, bf16[64,6272]{1,0:T(8,128)(2,1)S(1)}, u32[]{:S(2)}, u32[]{:S(2)}) collective-permute-start(bf16[64,6272]{1,0:T(8,128)(2,1)} %reduce-scatter.2.cloned.1.call-done), channel_id=1, source_target_pairs={{0,32},{32,0},{1,33},{33,1},{2,34},{34,2},{3,35},{35,3},{4,36},{36... | collective-permute-start | bytes 2408456 | tf_op jit(solution)/shard_map/ppermute | solution.py:48
  422.4 5.1 %collective-permute-start.8 = (f32[64,6272]{1,0:T(8,128)S(1)}, f32[64,6272]{1,0:T(8,128)}, u32[]{:S(2)}, u32[]{:S(2)}) collective-permute-start(f32[64,6272]{1,0:T(8,128)S(1)} %convert_add_fusion), channel_id=1, source_target_pairs={{0,16},{16,0},{1,17},{17,1},{2,18},{18,2},{3,19},{19,3},{4,20},{20... | collective-permute-start | bytes 4816904 | tf_op jit(solution)/shard_map/ppermute | solution.py:44
  431.0 1.9 copy-start.1
Sparse Core Ops, SparseCore 0:
  11.4 96.4 all-gather.1
  307.0 93.8 reduce-scatter.1
